TPU v7x, 32 devices: a whole 2x2x4 slice. The times are simulated.
32 devices in a mesh: dp: 8 (over y, x, core), mp: 4 (over z).
Axes of the slice: x: 2, y: 2, z: 4, core: 2. Of those that a mesh axis runs over, the one named last changes fastest.
Arguments:
- tokens: bfloat16 [16384, 768], P('dp'), may hold values from -6 to 6
- segments: int32 [16, 1024], P('dp'), may hold values from 0 to 7, never falling along the last dimension, each value on 1 to 512 neighbouring positions
- norm_gains: float32 [2, 768], replicated, may hold values from 0.1 to 1.9
- norm_shifts: float32 [2, 768], replicated, may hold values from -1.75 to 1.75
- qkv_weight: float32 [3, 768, 768], P(None, None, 'mp'), may hold values from -0.21875 to 0.21875
- qv_bias: float32 [2, 768], P(None, 'mp'), may hold values from -0.625 to 0.625
- out_weight: float32 [768, 768], P('mp'), may hold values from -1.75 to 1.75
- out_biases: float32 [2, 768], replicated, may hold values from -1.75 to 1.75
- up_weight: float32 [768, 3072], P(None, 'mp'), may hold values from -0.21875 to 0.21875
- up_bias: float32 [3072], P('mp'), may hold values from -3 to 3
- down_weight: float32 [3072, 768], P('mp'), may hold values from -0.109375 to 0.109375
- cotangent: bfloat16 [16384, 768], P('dp'), may hold values from -6 to 6
Outputs:
- result: bfloat16 [16384, 768], P('dp')
- token_grad: float32 [16384, 768], P('dp')
- gains_grad: float32 [2, 768], replicated
- shifts_grad: float32 [2, 768], replicated
- qkv_grad: float32 [3, 768, 768], P(None, None, 'mp')
- qv_bias_grad: float32 [2, 768], P(None, 'mp')
- out_weight_grad: float32 [768, 768], P('mp')
- out_biases_grad: float32 [2, 768], replicated
- up_grad: float32 [768, 3072], P(None, 'mp')
- up_bias_grad: float32 [3072], P('mp')
- down_grad: float32 [3072, 768], P('mp')
Inputs may be any that keep to these rules, and one draw needn't show every extreme that they name: `segments`: within each packed row the document numbers never fall, every number of 0 to 7 occurs, each document has 1 to 512 tokens, and some document has exactly 512.
All inputs are finite; a program needn't handle non-finite values.
Results may differ from a plain program's by a relative error of at most 0.012.
The roundings to bfloat16 on the way count: a program that leaves them out, or rounds other values in their place, can miss the bound.
Values sent between devices are 32-bit elements; how exact they have to be, the bound alone decides.
A program may use at most 192 MiB of HBM per device.

v0:
```python
from functools import partial

import jax
import jax.numpy as jnp
from jax import lax
from jax.sharding import PartitionSpec as P

HEAD_DIM = 64


NORM_EPSILON = 1e-06
MASKED_SCORE = -1000000000.0


def standardize(values):
    centered = values - jnp.mean(values, -1, keepdims=True)
    inv_std = lax.rsqrt(jnp.mean(centered * centered, -1, keepdims=True) + NORM_EPSILON)
    return (centered * inv_std, inv_std)


def norm_back(grad_in, normed, inv_std, gain):
    scaled = grad_in * gain
    return inv_std * (
        scaled
        - jnp.mean(scaled, -1, keepdims=True)
        - normed * jnp.mean(scaled * normed, -1, keepdims=True)
    )


def contract_rows(left, right):
    return lax.dot_general(
        left, right, (((0,), (0,)), ((), ())), preferred_element_type=jnp.float32
    )


def contract_cols(left, right):
    return lax.dot_general(
        left, right, (((1,), (1,)), ((), ())), preferred_element_type=jnp.float32
    )


def score_block(query_block, keys_row, doc_block, doc_row):
    scores = jnp.einsum(
        "qhd,khd->hqk", query_block, keys_row, preferred_element_type=jnp.float32
    ) * HEAD_DIM ** (-0.5)
    same_doc = doc_block[:, None] == doc_row[None, :]
    return jnp.where(same_doc[None], scores, MASKED_SCORE)


def attend_row(pieces):
    queries, keys_row, values_row, doc_row = pieces
    length = doc_row.shape[0]
    width = min(512, length)
    count = length // width
    heads_here = queries.shape[1]

    def per_block(block_pieces):
        query_block, doc_block = block_pieces
        scores = score_block(query_block, keys_row, doc_block, doc_row)
        highest = jnp.max(scores, -1, keepdims=True)
        exponent = jnp.exp(scores - highest)
        total = jnp.sum(exponent, -1, keepdims=True)
        probs = (exponent / total).astype(jnp.bfloat16)
        output = jnp.einsum("hqk,khd->qhd", probs, values_row, preferred_element_type=jnp.float32)
        return (output.astype(jnp.bfloat16), (highest + jnp.log(total))[:, :, 0])

    outputs, log_sums = lax.map(
        per_block,
        (queries.reshape(count, width, heads_here, HEAD_DIM), doc_row.reshape(count, width)),
    )
    return (outputs.reshape(length, heads_here, HEAD_DIM), log_sums)


def attend_row_back(pieces):
    queries, keys_row, values_row, doc_row, log_sums, out_grad = pieces
    length = doc_row.shape[0]
    width = min(512, length)
    count = length // width
    heads_here = queries.shape[1]
    score_scale = HEAD_DIM ** (-0.5)

    def per_block(running, block_pieces):
        key_grad, value_grad = running
        query_block, doc_block, log_block, grad_block = block_pieces
        scores = score_block(query_block, keys_row, doc_block, doc_row)
        probs = jnp.exp(scores - log_block[:, :, None])
        value_grad = value_grad + jnp.einsum(
            "hqk,qhd->khd",
            probs.astype(jnp.bfloat16),
            grad_block,
            preferred_element_type=jnp.float32,
        )
        prob_grad = jnp.einsum(
            "qhd,khd->hqk", grad_block, values_row, preferred_element_type=jnp.float32
        )
        inner_sum = jnp.sum(probs * prob_grad, -1, keepdims=True)
        score_grad = (probs * (prob_grad - inner_sum)).astype(jnp.bfloat16)
        query_grad = (
            jnp.einsum("hqk,khd->qhd", score_grad, keys_row, preferred_element_type=jnp.float32)
            * score_scale
        )
        key_grad = (
            key_grad
            + jnp.einsum(
                "hqk,qhd->khd", score_grad, query_block, preferred_element_type=jnp.float32
            )
            * score_scale
        )
        return ((key_grad, value_grad), query_grad.astype(jnp.bfloat16))

    zeros = jnp.zeros((length, heads_here, HEAD_DIM), jnp.float32)
    block_shape = (count, width, heads_here, HEAD_DIM)
    (key_grad, value_grad), query_grads = lax.scan(
        per_block,
        (zeros, zeros),
        (
            queries.reshape(block_shape),
            doc_row.reshape(count, width),
            log_sums,
            out_grad.reshape(block_shape),
        ),
    )
    return (
        query_grads.reshape(length, heads_here, HEAD_DIM),
        key_grad.astype(jnp.bfloat16),
        value_grad.astype(jnp.bfloat16),
    )


def body(
    tokens,
    segments,
    norm_gains,
    norm_shifts,
    qkv_weight,
    qv_bias,
    out_weight,
    out_biases,
    up_weight,
    up_bias,
    down_weight,
    cotangent,
):
    rows_here, length = segments.shape
    local_width = qkv_weight.shape[2]
    heads_here = local_width // HEAD_DIM
    token_count = rows_here * length
    row_shape = (rows_here, length, heads_here, HEAD_DIM)
    residual = tokens.astype(jnp.float32)
    normed_one, inv_one = standardize(residual)
    hidden_one = (normed_one * norm_gains[0] + norm_shifts[0]).astype(jnp.bfloat16)
    weights_qkv = qkv_weight.astype(jnp.bfloat16)
    queries = (
        jnp.dot(hidden_one, weights_qkv[0], preferred_element_type=jnp.float32) + qv_bias[0]
    ).astype(jnp.bfloat16)
    keys_all = jnp.dot(hidden_one, weights_qkv[1], preferred_element_type=jnp.float32).astype(
        jnp.bfloat16
    )
    values_all = (
        jnp.dot(hidden_one, weights_qkv[2], preferred_element_type=jnp.float32) + qv_bias[1]
    ).astype(jnp.bfloat16)
    queries_rows = queries.reshape(row_shape)
    keys_rows = keys_all.reshape(row_shape)
    values_rows = values_all.reshape(row_shape)
    attended, log_sums = lax.map(attend_row, (queries_rows, keys_rows, values_rows, segments))
    attended = attended.reshape(token_count, local_width)
    out_low = out_weight.astype(jnp.bfloat16)
    attn_total = lax.psum(jnp.dot(attended, out_low, preferred_element_type=jnp.float32), "mp")
    mixed_res = residual + attn_total + out_biases[0]
    normed_two, inv_two = standardize(mixed_res)
    hidden_two = (normed_two * norm_gains[1] + norm_shifts[1]).astype(jnp.bfloat16)
    up_low = up_weight.astype(jnp.bfloat16)
    pre_act = jnp.dot(hidden_two, up_low, preferred_element_type=jnp.float32) + up_bias
    activated = jax.nn.gelu(pre_act, approximate=True).astype(jnp.bfloat16)
    down_low = down_weight.astype(jnp.bfloat16)
    mlp_total = lax.psum(jnp.dot(activated, down_low, preferred_element_type=jnp.float32), "mp")
    result = mixed_res + mlp_total + out_biases[1]
    grad_out = cotangent.astype(jnp.float32)
    down_grad = contract_rows(activated, cotangent)
    act_grad = contract_cols(cotangent, down_low)
    _, gelu_back = jax.vjp(partial(jax.nn.gelu, approximate=True), pre_act)
    pre_grad = gelu_back(act_grad)[0].astype(jnp.bfloat16)
    up_grad = contract_rows(hidden_two, pre_grad)
    up_bias_grad = jnp.sum(pre_grad.astype(jnp.float32), 0)
    hidden_two_grad = lax.psum(contract_cols(pre_grad, up_low), "mp")
    mixed_grad = grad_out + norm_back(hidden_two_grad, normed_two, inv_two, norm_gains[1])
    gain_two = jnp.sum(hidden_two_grad * normed_two, 0)
    shift_two = jnp.sum(hidden_two_grad, 0)
    mixed_low = mixed_grad.astype(jnp.bfloat16)
    out_weight_grad = contract_rows(attended, mixed_low)
    attended_grad = contract_cols(mixed_low, out_low).astype(jnp.bfloat16)
    query_grad, key_grad, value_grad = lax.map(
        attend_row_back,
        (
            queries_rows,
            keys_rows,
            values_rows,
            segments,
            log_sums,
            attended_grad.reshape(row_shape),
        ),
    )
    query_grad = query_grad.reshape(token_count, local_width)
    key_grad = key_grad.reshape(token_count, local_width)
    value_grad = value_grad.reshape(token_count, local_width)
    qkv_grad = jnp.stack(
        [
            contract_rows(hidden_one, query_grad),
            contract_rows(hidden_one, key_grad),
            contract_rows(hidden_one, value_grad),
        ]
    )
    qv_bias_grad = jnp.stack(
        [jnp.sum(query_grad.astype(jnp.float32), 0), jnp.sum(value_grad.astype(jnp.float32), 0)]
    )
    hidden_one_part = (
        contract_cols(query_grad, weights_qkv[0])
        + contract_cols(key_grad, weights_qkv[1])
        + contract_cols(value_grad, weights_qkv[2])
    )
    hidden_one_grad = lax.psum(hidden_one_part, "mp")
    token_grad = mixed_grad + norm_back(hidden_one_grad, normed_one, inv_one, norm_gains[0])
    gains_grad = jnp.stack([jnp.sum(hidden_one_grad * normed_one, 0), gain_two])
    shifts_grad = jnp.stack([jnp.sum(hidden_one_grad, 0), shift_two])
    out_biases_grad = jnp.stack([jnp.sum(mixed_grad, 0), jnp.sum(grad_out, 0)])
    (
        qkv_grad,
        qv_bias_grad,
        out_weight_grad,
        gains_grad,
        shifts_grad,
        out_biases_grad,
        up_grad,
        up_bias_grad,
        down_grad,
    ) = lax.psum(
        (
            qkv_grad,
            qv_bias_grad,
            out_weight_grad,
            gains_grad,
            shifts_grad,
            out_biases_grad,
            up_grad,
            up_bias_grad,
            down_grad,
        ),
        "dp",
    )
    return (
        result.astype(jnp.bfloat16),
        token_grad,
        gains_grad,
        shifts_grad,
        qkv_grad,
        qv_bias_grad,
        out_weight_grad,
        out_biases_grad,
        up_grad,
        up_bias_grad,
        down_grad,
    )


def solution(mesh):
    in_specs = (
        P("dp", None),
        P("dp", None),
        P(),
        P(),
        P(None, None, "mp"),
        P(None, "mp"),
        P("mp", None),
        P(),
        P(None, "mp"),
        P("mp"),
        P("mp", None),
        P("dp", None),
    )
    out_specs = (
        P("dp", None),
        P("dp", None),
        P(),
        P(),
        P(None, None, "mp"),
        P(None, "mp"),
        P("mp", None),
        P(),
        P(None, "mp"),
        P("mp"),
        P("mp", None),
    )
    return jax.shard_map(body, mesh=mesh, in_specs=in_specs, out_specs=out_specs, check_vma=False)
```

profile of v0, /device:TPU:0, one launch (start us, length us, event | category | flops | bytes accessed | tf_op | source)
XLA Modules:
  0.0 1219.5 jit_solution(13307879756691009133)
XLA Ops:
  8.1 2.5 convert_reduce_fusion
  10.7 2.9 fusion.56
  19.4 4.0 fusion.65
  23.4 2.6 reshape.201
  28.8 47.0 %while.54 = (s32[]{:T(128)}, bf16[2,1024,3,64]{1,0,3,2:T(2,128)(2,1)S(1)}, f32[2,2,3,512]{3,2,1,0:T(4,128)}, bf16[2,1024,3,64]{1,3,2,0:T(8,128)(2,1)}, s32[2,102...) while((s32[]{:T(128)}, ...), condition=%wide.region_7.8_spmd, body=%wide.region_2.7_spmd.sunk | while | flops 422148608 | bytes 28561744 | solution.py:165
  33.2 11.3 while.57
  36.7 2.1 fusion.159
  42.4 2.1 fusion.159
  46.9 5.4 dynamic_update_slice.44
  56.6 11.3 while.57
  60.2 2.1 fusion.159
  65.8 2.1 fusion.159
  70.3 5.4 dynamic_update_slice.44
  77.6 5.0 fusion.83
  83.6 224.7 %all-reduce.8.cloned.1.call-done = f32[2048,768]{1,0:T(8,128)} async-done(((f32[2048,768]{1,0:T(8,128)}), f32[2048,768]{1,0:T(8,128)}) %all-reduce.8.cloned.1.call-update) | async-done | bytes 6291472 | tf_op jit(solution)/shard_map/psum | solution.py:168
  308.3 3.7 fusion.89
  316.4 2.8 fusion.78
  319.2 7.0 convert_reduce_fusion.2
  327.8 4.5 fusion.76
  332.5 10.2 fusion.72
  342.7 211.7 %all-reduce.10.cloned.1.call-done = f32[2048,768]{1,0:T(8,128)} async-done(((f32[2048,768]{1,0:T(8,128)}), f32[2048,768]{1,0:T(8,128)}) %all-reduce.10.cloned.1.call-update) | async-done | bytes 6291472 | tf_op jit(solution)/shard_map/psum | solution.py:185
  554.4 6.6 multiply_reduce_fusion.1
  561.0 5.9 fusion.88
  566.9 2.7 copy-done.4
  572.4 71.6 %while.56 = (s32[]{:T(128)}, bf16[2,1024,3,64]{3,2,1,0:T(4,128)(2,1)}, bf16[2,1024,3,64]{1,3,2,0:T(8,128)(2,1)}, bf16[2,1024,3,64]{1,3,2,0:T(8,128)(2,1)}, bf16[...) while((s32[]{:T(128)}, ...), condition=%wide.region_19.20_spmd, body=%wide.region_15.19_spmd.sunk | while | flops 1032321536 | bytes 73437736 | solution.py:192
  580.2 22.3 %while.58 = (s32[]{:T(128)}, f32[1024,3,64]{0,2,1:T(8,128)S(1)}, f32[1024,3,64]{0,2,1:T(8,128)}, bf16[2,512,3,64]{1,3,2,0:T(8,128)(2,1)S(1)}, bf16[2,512,3,64]{1...) while((s32[]{:T(128)}, f32[1024,3,64]{0,2,1:T(8,128)S(1)}, ...), condition=%wide.region_18.18_spmd.clone, body=%wide.region_16.17_spmd.clone.sunk | while | flops 1031928320 | bytes 60940512 | solution.py:113
  583.1 2.0 fusion.153
  585.1 2.5 multiply_reduce_fusion.7
  594.2 2.0 fusion.153
  596.2 2.5 multiply_reduce_fusion.7
  606.2 2.1 bitcast_dynamic-update-slice_fusion.11
  615.9 22.3 %while.58 = (s32[]{:T(128)}, f32[1024,3,64]{0,2,1:T(8,128)S(1)}, f32[1024,3,64]{0,2,1:T(8,128)}, bf16[2,512,3,64]{1,3,2,0:T(8,128)(2,1)S(1)}, bf16[2,512,3,64]{1...) while((s32[]{:T(128)}, f32[1024,3,64]{0,2,1:T(8,128)S(1)}, ...), condition=%wide.region_18.18_spmd.clone, body=%wide.region_16.17_spmd.clone.sunk | while | flops 1031928320 | bytes 60940512 | solution.py:113
  620.8 2.5 multiply_reduce_fusion.7
  632.0 2.5 multiply_reduce_fusion.7
  641.9 2.1 bitcast_dynamic-update-slice_fusion.11
  644.0 2.1 copy.50
  649.3 3.7 copy.49
  657.6 3.8 add_add_fusion
  661.5 7.1 fusion.92
  668.6 7.9 fusion.85
  680.4 2.2 convert_reduce_fusion.3
  685.9 401.4 %all-reduce.14.cloned.1.call-done = (f32[2048,768]{1,0:T(8,128)}, f32[2048,768]{1,0:T(8,128)}) async-done(((f32[2048,768]{1,0:T(8,128)}, f32[2048,768]{1,0:T(8,128)}), (f32[2048,768]{1,0:T(8,128)}, f32[2048,768]{1,0:T(8,128)})) %all-reduce.14.cloned.1.call-update) | async-done | bytes 12582928 | tf_op jit(solution)/shard_map/psum | solution.py:176
  1087.4 4.9 fusion.55
  1092.4 26.0 %all-reduce = (f32[2,768]{1,0:T(2,128)}, f32[2,768]{1,0:T(2,128)}, f32[2,192]{1,0:T(2,128)}, f32[2,768]{1,0:T(2,128)}, f32[768]{0:T(1024)}) all-reduce(f32[2,768]{1,0:T(2,128)S(1)} %pad_maximum_fusion.1, f32[2,768]{1,0:T(2,128)S(1)} %pad_maximum_fusion.2, ...), channel_id=1, replica_groups=mesh['dp'=8,'mp'=4] {'dp'}, use_global_device_ids=true, to_apply=%region_25.26 | all-reduce | flops 5760 | bytes 46080 | tf_op jit(solution)/shard_map/psum | solution.py:236
  1118.4 7.5 add_convert_fusion
  1125.9 7.7 fusion.54
  1133.6 71.2 %all-reduce.12.cloned.1.call-done = (f32[3,768,192]{1,2,0:T(8,128)}, f32[192,768]{1,0:T(8,128)}, f32[768,768]{1,0:T(8,128)}, f32[768,768]{1,0:T(8,128)}) async-done(((f32[3,768,192]{1,2,0:T(8,128)}, f32[192,768]{1,0:T(8,128)}, f32[768,768]{1,0:T(8,128)}, f32[768,768]{1,0:T(8,128)}), (f32[3,768,192]{1,2,0:T(8,128)}, f32[192,768]{1,0:T(8,128)}, f32[768,768]{1,0:T(8,128)}, ...) | async-done | bytes 7077904 | tf_op jit(solution)/shard_map/psum | solution.py:236
  1204.8 2.9 copy.130
  (296 shorter events, 120.7 us)
Async XLA Ops:
  7.2 7.3 copy-start.1
  7.2 6.6 copy-start.42
  7.2 6.6 copy-start.43
  7.2 301.1 %all-reduce.8.cloned.1.call-start = ((), (), s32[]{:S(2)}) async-start(), calls=%async_computation | async-start | bytes 12582912 | tf_op jit(solution)/shard_map/psum | solution.py:168
  7.3 6.4 copy-start.27
  10.7 6.3 copy-start.29
  13.7 3.3 copy-start.31
  13.8 3.2 copy-start.19
  19.4 9.4 copy-start.28
  77.6 5.4 copy-start.44
  77.6 230.7 %copy-start.2 = (bf16[2048,768]{1,0:T(8,128)(2,1)S(1)}, bf16[2048,768]{1,0:T(8,128)(2,1)}, u32[]{:S(2)}) copy-start(bf16[2048,768]{1,0:T(8,128)(2,1)} %param.20) | copy-start | bytes 9437188
  82.6 471.8 %all-reduce.10.cloned.1.call-start = ((), (), s32[]{:S(2)}) async-start(), calls=%async_computation.1 | async-start | bytes 12582912 | tf_op jit(solution)/shard_map/psum | solution.py:185
  312.8 3.5 copy-start.46
  316.4 2.8 copy-start.22
  316.4 2.8 copy-start.47
  316.4 2.8 copy-start.48
  319.2 7.0 copy-start.51
  332.4 755.0 %all-reduce.14.cloned.1.call-start = ((), (), s32[]{:S(2)}) async-start(), calls=%async_computation.3 | async-start | bytes 25165824 | tf_op jit(solution)/shard_map/psum | solution.py:176
  554.4 6.6 copy-start.10
  561.0 8.6 copy-start.26
  566.9 5.5 copy-start.8
  580.2 2.8 copy-start.11
  591.3 2.8 copy-start.11
  615.9 2.9 copy-start.11
  627.1 2.8 copy-start.11
  644.0 5.3 copy-start.16
  653.0 3.4 copy-start.20
  661.4 7.1 copy-start.49
  661.4 543.4 %all-reduce.12.cloned.1.call-start = ((), (), s32[]{:S(2)}) async-start(), calls=%async_computation.2 | async-start | bytes 14155776 | tf_op jit(solution)/shard_map/psum | solution.py:236
  661.5 7.1 copy-start.23
  668.6 7.9 copy-start.6
  677.4 3.0 copy-start.17
  677.4 5.2 slice-start
  677.4 5.2 copy-start.14
  678.2 4.3 slice-start.1
  682.6 3.1 copy-start.37
  682.6 3.1 copy-start.36
  682.6 3.1 copy-start.41
  682.6 3.1 copy-start.40
  682.6 404.7 %copy-start.3 = (bf16[2048,768]{1,0:T(8,128)(2,1)S(1)}, bf16[2048,768]{1,0:T(8,128)(2,1)}, u32[]{:S(2)}) copy-start(bf16[2048,768]{1,0:T(8,128)(2,1)} %param.20) | copy-start | bytes 9437188
  682.6 404.7 %copy-start.30 = (f32[2048]{0:T(1024)S(1)}, f32[2048]{0:T(1024)}, u32[]{:S(2)}) copy-start(f32[2048]{0:T(1024)} %copy-done.29) | copy-start | bytes 24580
  682.7 404.7 %copy-start.32 = (f32[2048]{0:T(1024)S(1)}, f32[2048]{0:T(1024)}, u32[]{:S(2)}) copy-start(f32[2048]{0:T(1024)} %copy-done.31) | copy-start | bytes 24580
  682.7 404.7 %copy-start.34 = (f32[768]{0:T(1024)S(1)}, f32[768]{0:T(1024)}, u32[]{:S(2)}) copy-start(f32[768]{0:T(1024)} %copy-done.33) | copy-start | bytes 9220
  684.3 408.1 %copy-start.45 = (f32[768]{0:T(1024)S(1)}, f32[768]{0:T(1024)}, u32[]{:S(2)}) copy-start(f32[768]{0:T(1024)} %get-tuple-element.415) | copy-start | bytes 9220
  684.3 434.0 %copy-start.38 = (f32[768]{0:T(1024)S(1)}, f32[768]{0:T(1024)}, u32[]{:S(2)}) copy-start(f32[768]{0:T(1024)} %get-tuple-element.307) | copy-start | bytes 9220
  1118.4 7.5 copy-start.9
  1204.8 4.9 copy-start.25
  1204.8 6.3 copy-start.24
  (17 other events, 29.3 us)
Sparse Core Ops, SparseCore 0:
  82.7 225.5 all-reduce.7
  332.5 221.7 all-reduce.9
  661.6 425.7 all-reduce.13
  1092.1 112.7 all-reduce.11
where the time goes:
time: 1230 us; the launch traced here: 1220 us
  waiting for transfers between devices  909 us (74%)
  matrix products  107 us (9%)
  local copies, waits for them, and re-layouts  86.9 us (7%)
  other arithmetic  74.4 us (6%)
  blocking collectives  26 us (2%)
  between operations  15 us (1%)
    psum x1, waiting for transfers between devices, body(): lax.psum(jnp.dot(activated, down_low, preferred_element_type=jnp.float32)...  401 us
    psum x1, waiting for transfers between devices, body(): lax.psum(jnp.dot(attended, out_low, preferred_element_type=jnp.float32),...  225 us
    psum x1, waiting for transfers between devices, body(): hidden_two_grad = lax.psum(contract_cols(pre_grad, up_low), 'mp')  212 us
    psum x1, waiting for transfers between devices, body(): lax.psum((qkv_grad, qv_bias_grad, out_weight_grad, gains_grad, shifts_gra...  71.2 us
    psum x1, blocking collectives, body(): lax.psum((qkv_grad, qv_bias_grad, out_weight_grad, gains_grad, shifts_gra...  26 us
  transfers between devices with their start and end apart: 4, of which 4 were waited for; matrix products, arithmetic and copies ran while one was open for 5% of the time, Pallas kernels for 0%

commit v1 on v0

v1 whole, which is shorter than its diff:
```python
from functools import partial

import jax
import jax.numpy as jnp
from jax import lax
from jax.experimental import pallas as pl
from jax.experimental.pallas import tpu as pltpu
from jax.sharding import PartitionSpec as P

F32 = jnp.float32
BF = jnp.bfloat16
HEAD_DIM = 64
NORM_EPSILON = 1e-06
BIG = 1e30
LOG2E = 1.4426950408889634
SAFE_SCORE = 60.0
REACH = 512
TILE = 256
EXTRA = 16
FWD_UNROLL = 4
BWD_UNROLL = 3

NN = (((1,), (0,)), ((), ()))
NT = (((1,), (1,)), ((), ()))
TN = (((0,), (0,)), ((), ()))
WHOLE = pl.BlockSpec(memory_space=pltpu.VMEM)
SCALARS = pl.BlockSpec(memory_space=pltpu.SMEM)


def dot(left, right, dims):
    return lax.dot_general(left, right, dims, preferred_element_type=F32)


def params(mib=56):
    return pltpu.CompilerParams(vmem_limit_bytes=mib * 2**20)


def standardize(values):
    centered = values - jnp.mean(values, -1, keepdims=True)
    inv_std = lax.rsqrt(jnp.mean(centered * centered, -1, keepdims=True) + NORM_EPSILON)
    return centered * inv_std, inv_std


def norm_back(grad_in, normed, inv_std, gain):
    scaled = grad_in * gain
    return inv_std * (
        scaled
        - jnp.mean(scaled, -1, keepdims=True)
        - normed * jnp.mean(scaled * normed, -1, keepdims=True)
    )


def shape_of(shape, dtype):
    return jax.ShapeDtypeStruct(shape, dtype)


def cast_kernel(in_ref, out_ref):
    out_ref[...] = in_ref[...].astype(BF)


def cast_low(array):
    rows, width = array.shape
    block = pl.BlockSpec((256, width), lambda i: (i, 0))
    return pl.pallas_call(
        cast_kernel,
        grid=(rows // 256,),
        in_specs=[block],
        out_specs=block,
        out_shape=shape_of(array.shape, BF),
    )(array)


def attend_kernel(
    x_ref, seg_ref, gain_ref, shift_ref, w_ref, b_ref,
    h1_ref, qt_ref, kt_ref, vt_ref, ot_ref, lse_ref,
    qx, kx, vx, kn,
):
    length, width = x_ref.shape
    heads = width // HEAD_DIM
    normed, _ = standardize(x_ref[...].astype(F32))
    h1_ref[...] = (normed * gain_ref[0:1, :] + shift_ref[0:1, :]).astype(BF)
    for j, out in enumerate((qt_ref, kt_ref, vt_ref)):
        value = dot(w_ref[j * width : (j + 1) * width, :], h1_ref[...], NT)
        if j != 1:
            value = value + b_ref[j * width : (j + 1) * width, :]
        value = value.astype(BF)
        if j == 0:
            value = value * jnp.asarray(HEAD_DIM**-0.5, BF)
        out[...] = value
    row = lax.broadcasted_iota(jnp.int32, (EXTRA, length), 0)
    same = row == seg_ref[0]
    for u in range(FWD_UNROLL):
        qx[u, HEAD_DIM:, :] = jnp.where(same | (row >= 8), 0.0, -BIG).astype(BF)
        kx[u, HEAD_DIM:, :] = jnp.where(same, 1.0, 0.0).astype(BF)
        vx[u, HEAD_DIM:, :] = jnp.ones((EXTRA, length), BF)

    def load(h, u):
        rows = pl.ds(pl.multiple_of(h * HEAD_DIM, HEAD_DIM), HEAD_DIM)
        qx[u, :HEAD_DIM, :] = qt_ref[rows, :]
        kx[u, :HEAD_DIM, :] = kt_ref[rows, :]
        vx[u, :HEAD_DIM, :] = vt_ref[rows, :]
        kn[u] = kx[u].T

    def norm_bound(ref, u):
        value = ref[u, :HEAD_DIM, :].astype(F32)
        return jnp.max(jnp.sum(value * value, 0, keepdims=True))

    def head(h, u, safe):
        rows = pl.ds(pl.multiple_of(h * HEAD_DIM, HEAD_DIM), HEAD_DIM)
        for t in range(length // TILE):
            low, high = max(0, t * TILE - REACH), min(length, (t + 1) * TILE + REACH)
            cols = slice(t * TILE, (t + 1) * TILE)
            if safe:
                highest = jnp.full((1, TILE), -BIG, F32)
                for k in range(low, high, TILE):
                    scores = dot(kn[u, k : k + TILE, :], qx[u, :, cols], NN)
                    highest = jnp.maximum(highest, jnp.max(scores, 0, keepdims=True))
            probs = []
            for k in range(low, high, TILE):
                scores = dot(kn[u, k : k + TILE, :], qx[u, :, cols], NN)
                if safe:
                    scores = scores - highest
                probs.append(jnp.exp2(scores * LOG2E).astype(BF))
            out = dot(vx[u, :, low:high], jnp.concatenate(probs, 0), NN)
            total = out[HEAD_DIM : HEAD_DIM + 1, :]
            ot_ref[rows, cols] = (out[:HEAD_DIM, :] * (1.0 / total)).astype(BF)
            log_sum = jnp.log(total)
            if safe:
                log_sum = log_sum + highest
            lse_ref[pl.ds(h, 1), cols] = log_sum

    def step(i, carry):
        bound = 0.0
        for u in range(FWD_UNROLL):
            load(i * FWD_UNROLL + u, u)
            bound = jnp.maximum(bound, norm_bound(qx, u) * norm_bound(kx, u))

        @pl.when(bound < SAFE_SCORE**2)
        def _():
            for u in range(FWD_UNROLL):
                head(i * FWD_UNROLL + u, u, False)

        @pl.when(jnp.logical_not(bound < SAFE_SCORE**2))
        def _():
            lax.fori_loop(0, FWD_UNROLL, lambda u, c: (head(i * FWD_UNROLL + u, u, True), c)[1], 0)

        return carry

    lax.fori_loop(0, heads // FWD_UNROLL, step, 0)


def attend(x, seg, gains, shifts, weights, bias):
    tokens, width = x.shape
    rows, _, length = seg.shape
    row = pl.BlockSpec((length, width), lambda r: (r, 0))
    col = pl.BlockSpec((width, length), lambda r: (0, r))
    return pl.pallas_call(
        attend_kernel,
        grid=(rows,),
        in_specs=[row, pl.BlockSpec((1, 1, length), lambda r: (r, 0, 0)), WHOLE, WHOLE, WHOLE, WHOLE],
        out_specs=[row, col, col, col, col, pl.BlockSpec((16, length), lambda r: (0, r))],
        out_shape=[shape_of((tokens, width), BF)]
        + [shape_of((width, tokens), BF)] * 4
        + [shape_of((16, tokens), F32)],
        scratch_shapes=[pltpu.VMEM((FWD_UNROLL, HEAD_DIM + EXTRA, length), BF)] * 3
        + [pltpu.VMEM((FWD_UNROLL, length, HEAD_DIM + EXTRA), BF)],
        compiler_params=params(),
        name="attend",
    )(x, seg, gains, shifts, weights, bias)


def split3(value):
    first = value.astype(BF)
    rest = value - first.astype(F32)
    second = rest.astype(BF)
    return first, second, (rest - second.astype(F32)).astype(BF)


def attend_back_kernel(
    start_ref, seg_ref, qt_ref, kt_ref, vt_ref, ot_ref, dt_ref, lse_ref,
    dq_ref, dk_ref, dv_ref,
    qx, kx, vx, dx, qn, dn, kn, acc,
):
    length = qt_ref.shape[1]
    heads = qt_ref.shape[0] // HEAD_DIM
    row = lax.broadcasted_iota(jnp.int32, (EXTRA, length), 0)
    same = row == seg_ref[0]
    key_extra = jnp.where(same | ((row >= 8) & (row < 11)), 1.0, 0.0).astype(BF)
    value_extra = jnp.where(row < 3, 1.0, 0.0).astype(BF)
    query_extra = jnp.where(same | (row >= 8), 0.0, -BIG)

    def three_rows(value, at):
        first, second, third = split3(value)
        out = jnp.where(row == at, first.astype(F32), 0.0)
        out = jnp.where(row == at + 1, second.astype(F32), out)
        return jnp.where(row == at + 2, third.astype(F32), out)

    def head(i, u):
        h = lax.rem(start_ref[0] + i, heads)
        rows = pl.ds(pl.multiple_of(h * HEAD_DIM, HEAD_DIM), HEAD_DIM)
        qx[u, :HEAD_DIM, :] = qt_ref[rows, :]
        kx[u, :HEAD_DIM, :] = kt_ref[rows, :]
        vx[u, :HEAD_DIM, :] = vt_ref[rows, :]
        dx[u, :HEAD_DIM, :] = dt_ref[rows, :]
        inner = jnp.sum(dt_ref[rows, :].astype(F32) * ot_ref[rows, :].astype(F32), 0, keepdims=True)
        qx[u, HEAD_DIM:, :] = (query_extra + three_rows(-lse_ref[pl.ds(h, 1), :], 8)).astype(BF)
        kx[u, HEAD_DIM:, :] = key_extra
        vx[u, HEAD_DIM:, :] = value_extra
        dx[u, HEAD_DIM:, :] = three_rows(-inner, 0).astype(BF)
        qn[u] = qx[u].T
        dn[u] = dx[u].T
        kn[u] = kx[u].T
        for t in range(length // TILE):
            low, high = max(0, t * TILE - REACH), min(length, (t + 1) * TILE + REACH)
            keys = slice(t * TILE, (t + 1) * TILE)
            probs, score_grads = [], []
            for q in range(low, high, TILE):
                prob = jnp.exp2(dot(qn[u, q : q + TILE, :], kx[u, :, keys], NN) * LOG2E)
                prob_grad = dot(dn[u, q : q + TILE, :], vx[u, :, keys], NN)
                probs.append(prob.astype(BF))
                score_grads.append((prob * prob_grad).astype(BF))
            probs = jnp.concatenate(probs, 0)
            score_grads = jnp.concatenate(score_grads, 0)
            dv_ref[rows, keys] = dot(dx[u, :HEAD_DIM, low:high], probs, NN).astype(BF)
            dk_ref[rows, keys] = dot(qx[u, :HEAD_DIM, low:high], score_grads, NN).astype(BF)
            part = dot(score_grads, kx[u, :HEAD_DIM, keys], NT)
            if t == 0:
                acc[u, low:high, :] = part
                if high < length:
                    acc[u, high:, :] = jnp.zeros((length - high, HEAD_DIM), F32)
            else:
                acc[u, low:high, :] += part
        dq_ref[rows, :] = (acc[u] * HEAD_DIM**-0.5).T.astype(BF)

    def step(i, carry):
        for u in range(BWD_UNROLL):
            head(i * BWD_UNROLL + u, u)
        return carry

    lax.fori_loop(0, heads // BWD_UNROLL, step, 0)


def attend_back(start, seg, qt, kt, vt, ot, dt, lse):
    width, tokens = qt.shape
    rows, _, length = seg.shape
    col = pl.BlockSpec((width, length), lambda r: (0, r))
    wide = HEAD_DIM + EXTRA
    return pl.pallas_call(
        attend_back_kernel,
        grid=(rows,),
        in_specs=[SCALARS, pl.BlockSpec((1, 1, length), lambda r: (r, 0, 0))]
        + [col] * 5
        + [pl.BlockSpec((16, length), lambda r: (0, r))],
        out_specs=[col] * 3,
        out_shape=[shape_of((width, tokens), BF)] * 3,
        scratch_shapes=[pltpu.VMEM((BWD_UNROLL, wide, length), BF)] * 4
        + [pltpu.VMEM((BWD_UNROLL, length, wide), BF)] * 3
        + [pltpu.VMEM((BWD_UNROLL, length, HEAD_DIM), F32)],
        compiler_params=params(),
        name="attend_back",
    )(start, seg, qt, kt, vt, ot, dt, lse)


def mix_kernel(x_ref, ot_ref, wo_ref, bias_ref, gain_ref, shift_ref, mixed_ref, h2_ref):
    mixed = x_ref[...].astype(F32) + dot(ot_ref[...], wo_ref[...], TN) + bias_ref[0:1, :]
    mixed_ref[...] = mixed
    normed, _ = standardize(mixed)
    h2_ref[...] = (normed * gain_ref[1:2, :] + shift_ref[1:2, :]).astype(BF)


def mix(x, ot, wo, biases, gains, shifts):
    tokens, width = x.shape
    row = pl.BlockSpec((TILE, width), lambda t: (t, 0))
    col = pl.BlockSpec((width, TILE), lambda t: (0, t))
    return pl.pallas_call(
        mix_kernel,
        grid=(tokens // TILE,),
        in_specs=[row, col, WHOLE, WHOLE, WHOLE, WHOLE],
        out_specs=[row, row],
        out_shape=[shape_of((tokens, width), F32), shape_of((tokens, width), BF)],
        compiler_params=params(),
        name="mix",
    )(x, ot, wo, biases, gains, shifts)


GELU_C = 0.7978845608028654
GELU_A = 0.044715


def gelu_both(pre):
    square = pre * pre
    half = 0.5 + 0.5 * jnp.tanh(pre * (GELU_C + (GELU_C * GELU_A) * square))
    act = pre * half
    slope = half + act * (1.0 - half) * (2.0 * GELU_C + (6.0 * GELU_C * GELU_A) * square)
    return act, slope


def mlp_kernel(
    me_ref, h2_ref, g_ref, up_ref, down_ref, bias_ref,
    res_ref, hg_ref, upg_ref, downg_ref, upbg_ref,
    up_low, down_low,
):
    j = pl.program_id(0)
    tokens = h2_ref.shape[0]
    up_low[...] = up_ref[0].astype(BF)
    down_low[...] = down_ref[0].astype(BF)

    def tiles(own):
        def tile(i, carry):
            rows = pl.ds(pl.multiple_of(i * TILE, TILE), TILE)
            h2 = h2_ref[rows, :]
            g = g_ref[rows, :]
            pre = dot(h2, up_low[...], NN) + bias_ref[0]
            act, slope = gelu_both(pre)
            act = act.astype(BF)
            pre_grad = (dot(g, down_low[...], NT) * slope).astype(BF)
            res = dot(act, down_low[...], NN)
            hg = dot(pre_grad, up_low[...], NT)
            if own:
                res_ref[rows, :] = res
                hg_ref[rows, :] = hg
                downg_ref[...] += dot(act, g, TN)
                upg_ref[...] += dot(h2, pre_grad, TN)
                upbg_ref[...] += jnp.sum(pre_grad.astype(F32), 0, keepdims=True)
            else:
                res_ref[rows, :] += res
                hg_ref[rows, :] += hg
            return carry

        lax.fori_loop(0, tokens // TILE, tile, 0)

    @pl.when(j == 0)
    def _():
        upg_ref[...] = jnp.zeros_like(upg_ref)
        downg_ref[...] = jnp.zeros_like(downg_ref)
        upbg_ref[...] = jnp.zeros_like(upbg_ref)
        tiles(True)

    @pl.when(j > 0)
    def _():
        tiles(False)


def mlp(me, h2, g, up, down, bias):
    tokens, width = h2.shape
    parts, _, ff = up.shape
    pick = lambda j, me: (lax.rem(me[0] + j, parts), 0, 0)
    return pl.pallas_call(
        mlp_kernel,
        grid_spec=pltpu.PrefetchScalarGridSpec(
            num_scalar_prefetch=1,
            grid=(parts,),
            in_specs=[
                WHOLE,
                WHOLE,
                pl.BlockSpec((1, width, ff), pick),
                pl.BlockSpec((1, ff, width), pick),
                pl.BlockSpec((1, 1, ff), pick),
            ],
            out_specs=[WHOLE] * 5,
            scratch_shapes=[pltpu.VMEM((width, ff), BF), pltpu.VMEM((ff, width), BF)],
        ),
        out_shape=[
            shape_of((tokens, width), F32),
            shape_of((tokens, width), F32),
            shape_of((width, ff), F32),
            shape_of((ff, width), F32),
            shape_of((1, ff), F32),
        ],
        compiler_params=params(),
        name="mlp",
    )(me, h2, g, up, down, bias)


def mix_back_kernel(
    me_ref, mixed_ref, res_ref, hg_ref, g_ref, ot_ref, wo_ref, bias_ref, gain_ref,
    result_ref, mg_ref, dt_ref, owg_ref, sums_ref,
):
    @pl.when(pl.program_id(0) == 0)
    def _():
        owg_ref[...] = jnp.zeros_like(owg_ref)
        sums_ref[...] = jnp.zeros_like(sums_ref)

    mixed = mixed_ref[...]
    g = g_ref[...].astype(F32)
    result_ref[...] = (mixed + res_ref[...] + bias_ref[1:2, :]).astype(BF)
    normed, inv_std = standardize(mixed)
    hg = hg_ref[...]
    mg = g + norm_back(hg, normed, inv_std, gain_ref[1:2, :])
    mg_ref[...] = mg
    low = mg.astype(BF)
    dt_ref[...] = dot(wo_ref[...], low, NT).astype(BF)
    owg_ref[...] += dot(ot_ref[...], low, NN)
    sums_ref[0:1, :] += jnp.sum(hg * normed, 0, keepdims=True)
    sums_ref[1:2, :] += jnp.sum(hg, 0, keepdims=True)
    sums_ref[2:3, :] += jnp.sum(mg, 0, keepdims=True)
    sums_ref[3:4, :] += jnp.sum(g, 0, keepdims=True)


def mix_back(me, mixed, res, hg, g, ot, wo, biases, gains, own):
    tokens, width = mixed.shape
    row = pl.BlockSpec((TILE, width), lambda t, me: (t, 0))
    return pl.pallas_call(
        mix_back_kernel,
        grid_spec=pltpu.PrefetchScalarGridSpec(
            num_scalar_prefetch=1,
            grid=(tokens // TILE,),
            in_specs=[row, row, row, row, pl.BlockSpec((own, TILE), lambda t, me: (me[0], t)), WHOLE, WHOLE, WHOLE],
            out_specs=[row, row, pl.BlockSpec((width, TILE), lambda t, me: (0, t)), WHOLE, WHOLE],
        ),
        out_shape=[
            shape_of((tokens, width), BF),
            shape_of((tokens, width), F32),
            shape_of((width, tokens), BF),
            shape_of((own, width), F32),
            shape_of((8, width), F32),
        ],
        compiler_params=params(),
        name="mix_back",
    )(me, mixed, res, hg, g, ot, wo, biases, gains)


def token_kernel(
    me_ref, dq_ref, dk_ref, dv_ref, dqo_ref, dko_ref, dvo_ref, w_ref, x_ref, h1_ref, mg_ref, gain_ref,
    tg_ref, qkvg_ref, sums_ref, rowsum_ref,
):
    @pl.when(pl.program_id(0) == 0)
    def _():
        qkvg_ref[...] = jnp.zeros_like(qkvg_ref)
        sums_ref[...] = jnp.zeros_like(sums_ref)
        rowsum_ref[...] = jnp.zeros_like(rowsum_ref)

    width = x_ref.shape[1]
    hg = dot(dq_ref[...], w_ref[:width, :], TN)
    hg += dot(dk_ref[...], w_ref[width : 2 * width, :], TN)
    hg += dot(dv_ref[...], w_ref[2 * width :, :], TN)
    normed, inv_std = standardize(x_ref[...].astype(F32))
    tg_ref[...] = mg_ref[...] + norm_back(hg, normed, inv_std, gain_ref[0:1, :])
    sums_ref[0:1, :] += jnp.sum(hg * normed, 0, keepdims=True)
    sums_ref[1:2, :] += jnp.sum(hg, 0, keepdims=True)
    h1 = h1_ref[...]
    ones = jnp.ones((h1.shape[0], 128), BF)
    for j, ref in enumerate((dqo_ref, dko_ref, dvo_ref)):
        qkvg_ref[j] += dot(ref[...], h1, NN)
        if j != 1:
            rowsum_ref[j // 2] += dot(ref[...], ones, NN)


def token_back(me, dq, dk, dv, weights, x, h1, mg, gains, own):
    tokens, width = x.shape
    row = pl.BlockSpec((TILE, width), lambda t, me: (t, 0))
    col = pl.BlockSpec((width, TILE), lambda t, me: (0, t))
    mine = pl.BlockSpec((own, TILE), lambda t, me: (me[0], t))
    return pl.pallas_call(
        token_kernel,
        grid_spec=pltpu.PrefetchScalarGridSpec(
            num_scalar_prefetch=1,
            grid=(tokens // TILE,),
            in_specs=[col, col, col, mine, mine, mine, WHOLE, row, row, row, WHOLE],
            out_specs=[row, WHOLE, WHOLE, WHOLE],
        ),
        out_shape=[
            shape_of((tokens, width), F32),
            shape_of((3, own, width), F32),
            shape_of((8, width), F32),
            shape_of((2, own, 128), F32),
        ],
        compiler_params=params(),
        name="token_back",
    )(me, dq, dk, dv, dq, dk, dv, weights, x, h1, mg, gains)


def body(
    dp_size,
    tokens,
    segments,
    norm_gains,
    norm_shifts,
    qkv_weight,
    qv_bias,
    out_weight,
    out_biases,
    up_weight,
    up_bias,
    down_weight,
    cotangent,
):
    width = tokens.shape[1]
    own = qkv_weight.shape[2]
    ff = up_weight.shape[1]
    me = lax.axis_index("mp").astype(jnp.int32).reshape(1)
    seg = segments.reshape(segments.shape[0], 1, segments.shape[1])
    slab = jnp.concatenate(
        [qkv_weight.transpose(0, 2, 1).reshape(3 * own, width), out_weight, up_weight, down_weight], 0
    )
    share = slab.shape[0] // dp_size
    piece = lax.dynamic_slice_in_dim(slab, lax.axis_index("dp") * share, share, 0)
    gathered = lax.all_gather(piece, ("mp", "dp"), tiled=True).reshape(-1, slab.shape[0], width)
    small = jnp.concatenate([jnp.pad(qv_bias, ((0, 0), (0, width - own))), up_bias.reshape(1, ff)], 0)
    smalls = lax.all_gather(small, "mp")
    parts = gathered.shape[0]
    qkv_t = gathered[:, : 3 * own].reshape(parts, 3, own, width).transpose(1, 0, 2, 3).reshape(3 * parts * own, width)
    weights = cast_low(qkv_t)
    wo = cast_low(gathered[:, 3 * own : 4 * own].reshape(parts * own, width))
    up = gathered[:, 4 * own : 4 * own + width]
    down = gathered[:, 4 * own + width :]
    full_bias = smalls[:, :2, :own].transpose(1, 0, 2).reshape(2, parts * own)
    bias = jnp.concatenate([full_bias[0], jnp.zeros_like(full_bias[0]), full_bias[1]]).reshape(-1, 1)
    h1, qt, kt, vt, ot, lse = attend(tokens, seg, norm_gains, norm_shifts, weights, bias)
    mixed, h2 = mix(tokens, ot, wo, out_biases, norm_gains, norm_shifts)
    res, hg, up_grad, down_grad, up_bias_grad = mlp(me, h2, cotangent, up, down, smalls[:, 2:3, :])
    result, mg, dt, out_weight_grad, sums_two = mix_back(
        me, mixed, res, hg, cotangent, ot, wo, out_biases, norm_gains, own
    )
    up_grad, down_grad, out_weight_grad, up_bias_grad = lax.psum(
        (up_grad, down_grad, out_weight_grad, up_bias_grad), "dp"
    )
    dq, dk, dv = attend_back(me * (own // HEAD_DIM), seg, qt, kt, vt, ot, dt, lse)
    token_grad, qkv_grad, sums_one, row_sums = token_back(
        me, dq, dk, dv, weights, tokens, h1, mg, norm_gains, own
    )
    qkv_grad, sums_one, sums_two, row_sums = lax.psum(
        (qkv_grad, sums_one[:2], sums_two[:4], row_sums[:, :, 0]), "dp"
    )
    return (
        result,
        token_grad,
        jnp.stack([sums_one[0], sums_two[0]]),
        jnp.stack([sums_one[1], sums_two[1]]),
        qkv_grad.transpose(0, 2, 1),
        row_sums,
        out_weight_grad,
        sums_two[2:4],
        up_grad,
        up_bias_grad.reshape(ff),
        down_grad,
    )


def solution(mesh):
    in_specs = (
        P("dp", None),
        P("dp", None),
        P(),
        P(),
        P(None, None, "mp"),
        P(None, "mp"),
        P("mp", None),
        P(),
        P(None, "mp"),
        P("mp"),
        P("mp", None),
        P("dp", None),
    )
    out_specs = (
        P("dp", None),
        P("dp", None),
        P(),
        P(),
        P(None, None, "mp"),
        P(None, "mp"),
        P("mp", None),
        P(),
        P(None, "mp"),
        P("mp"),
        P("mp", None),
    )
    return jax.shard_map(
        partial(body, mesh.shape["dp"]), mesh=mesh, in_specs=in_specs, out_specs=out_specs, check_vma=False
    )
```

time: 1230 us -> 566 us (0.46)
  waiting for transfers between devices: 909 us -> 240 us
  Pallas kernels: 0 us -> 227 us
  matrix products: 107 us -> 0 us
  other arithmetic: 74.4 us -> 3.77 us
  local copies, waits for them, and re-layouts: 86.9 us -> 40.2 us
  blocking collectives: 26 us -> 40.3 us
    psum x4 -> x1, waiting for transfers between devices: 909 us -> 83.8 us  [body(): lax.psum((qkv_grad, sums_one[:2], sums_two[:4], row_sums[:, :, 0]), 'dp')]
    pallas_call x0 -> x8, Pallas kernels: none -> 227 us  [the longest x1 64.4 us: mlp(): pl.pallas_call(mlp_kernel, grid_spec=pltpu.PrefetchScalarGridSpec(num_sca...]
    all_gather x0 -> x1, waiting for transfers between devices: none -> 157 us  [body(): lax.all_gather(piece, ('mp', 'dp'), tiled=True)]
    dot_general x46 -> x0, matrix products: 107 us -> none  [the longest x6 19.6 us: contract_cols(): lax.dot_general(left, right, (((1,), (1,)), ((), ())), preferred_element_...]
    reduce_sum x13 -> x0, other arithmetic: 37.9 us -> none  [the longest x4 7.03 us: per_block(): total = jnp.sum(exponent, -1, keepdims=True)]
    slice x3 -> x10, local copies, waits for them, and re-layouts: 2.15 us -> 24.9 us  [the longest x1 13.2 us: body(): down = gathered[:, 4 * own + width:]]
    dynamic_slice x22 -> x0, local copies, waits for them, and re-layouts: 17.9 us -> none  [the longest x14 14.8 us: body(): lax.map(attend_row, (queries_rows, keys_rows, values_rows, segments))]
    while x37 -> x0, local copies, waits for them, and re-layouts: 17.6 us -> none  [the longest x4 8.82 us: body(): lax.map(attend_row_back, (queries_rows, keys_rows, values_rows, segments,...]
  transfers between devices with their start and end apart: 4 -> 2, of which waited for: 4 -> 2; matrix products, arithmetic and copies ran while one was open for 5% -> 1% of each run, Pallas kernels for 0% -> 0%
where the time goes in v1:
time: 566 us; the launch traced here: 565 us
  waiting for transfers between devices  240 us (42%)
  Pallas kernels  227 us (40%)
  blocking collectives  40.3 us (7%)
  local copies, waits for them, and re-layouts  40.2 us (7%)
  between operations  14.2 us (3%)
    all_gather x1, waiting for transfers between devices, body(): lax.all_gather(piece, ('mp', 'dp'), tiled=True)  157 us
    psum x1, waiting for transfers between devices, body(): lax.psum((qkv_grad, sums_one[:2], sums_two[:4], row_sums[:, :, 0]), 'dp')  83.8 us
    pallas_call x1, Pallas kernels, mlp(): pl.pallas_call(mlp_kernel, grid_spec=pltpu.PrefetchScalarGridSpec(num_sca...  64.4 us
    pallas_call x1, Pallas kernels, attend_back(): pl.pallas_call(attend_back_kernel, grid=(rows,), in_specs=[SCALARS, pl.Bl...  60.3 us
    pallas_call x1, Pallas kernels, attend(): pl.pallas_call(attend_kernel, grid=(rows,), in_specs=[row, pl.BlockSpec((...  43.8 us
    psum x1, blocking collectives, body(): lax.psum((qkv_grad, sums_one[:2], sums_two[:4], row_sums[:, :, 0]), 'dp')  25.5 us
    pallas_call x1, Pallas kernels, token_back(): pl.pallas_call(token_kernel, grid_spec=pltpu.PrefetchScalarGridSpec(num_s...  20.1 us
    pallas_call x1, Pallas kernels, mix_back(): pl.pallas_call(mix_back_kernel, grid_spec=pltpu.PrefetchScalarGridSpec(nu...  16.7 us
  transfers between devices with their start and end apart: 2, of which 2 were waited for; matrix products, arithmetic and copies ran while one was open for 1% of the time, Pallas kernels for 0%

profile of v1, /device:TPU:0, one launch (start us, length us, event | category | flops | bytes accessed | tf_op | source)
XLA Modules:
  0.0 565.3 jit_solution(1429660041415144684)
XLA Ops:
  7.2 0.0 all-gather.4.cloned.1.call-start
  7.2 0.0 copy-start.6
  7.2 0.0 copy-start.4
  7.3 0.0 copy-start.8
  7.3 2.5 fusion.2
  9.8 0.0 all-gather.4.cloned.1.call-update
  9.8 0.0 all-reduce.5.cloned.1.call-start
  9.9 0.0 copy-done.6
  9.9 0.0 copy-done.4
  9.9 0.6 reshape.58.seg_ref
  10.5 0.0 copy-done.8
  10.5 14.7 %all-gather.1 = f32[4,3,768]{2,1,0:T(4,128)S(1)} all-gather(f32[1,3,768]{2,1,0:T(4,128)S(1)} %fusion.3), channel_id=2, replica_groups=mesh['dp'=8,'mp'=4] {'mp'}, dimensions={0}, use_global_device_ids=true | all-gather | bytes 46080 | tf_op jit(solution)/shard_map/all_gather | solution.py:500
  25.3 0.6 slice.73.bias_ref
  25.9 0.1 squeeze.9
  26.0 0.1 squeeze.10
  26.1 1.4 reshape.71.b_ref
  27.5 156.5 %all-gather.4.cloned.1.call-done = f32[9216,768]{1,0:T(8,128)} async-done(((f32[288,768]{1,0:T(8,128)}), f32[9216,768]{1,0:T(8,128)}) %all-gather.4.cloned.1.call-update) | async-done | bytes 28311568 | tf_op jit(solution)/shard_map/all_gather | solution.py:498
  184.0 3.2 slice.70
  187.2 6.4 %slice.66 = f32[4,576,768]{2,1,0:T(8,128)} slice(f32[4,2304,768]{2,1,0:T(8,128)} %bitcast.17), slice={[0:4], [0:576], [0:768]} | slice | bytes 14155776 | tf_op jit(solution)/shard_map/slice | solution.py:502
  193.6 13.2 %fusion.4 = (f32[4,768,768]{2,1,0:T(8,128)}, f32[4,768,768]{2,1,0:T(8,128)}) fusion(f32[4,2304,768]{2,1,0:T(8,128)} %bitcast.18), kind=kLoop, calls=%fused_computation.17 | loop fusion | bytes 37748736 | tf_op jit(solution)/shard_map/slice | solution.py:506
  206.7 3.4 shard_map.204.wo_ref
  210.2 6.4 %copy.26 = f32[3,4,192,768]{3,2,1,0:T(8,128)} copy(f32[3,4,192,768]{3,2,0,1:T(8,128)} %bitcast.15) | data formatting | bytes 14155776 | tf_op jit(solution)/shard_map/transpose | solution.py:502
  216.5 7.6 %shard_map.203.w_ref = bf16[2304,768]{1,0:T(8,128)(2,1)} custom-call(f32[2304,768]{1,0:T(8,128)} %bitcast.19), custom_call_target="tpu_custom_call" | custom-call | tf_op jit(solution)/shard_map/pallas_call | solution.py:64
  224.1 43.8 %attend.1 = (bf16[2048,768]{1,0:T(8,128)(2,1)}, bf16[768,2048]{1,0:T(8,128)(2,1)}, bf16[768,2048]{1,0:T(8,128)(2,1)}, bf16[768,2048]{1,0:T(8,128)(2,1)}, bf16[768,2048]{1,0:T(8,128)(2,1)}, /*index=5*/f32[16,2048]{1,0:T(8,128)}) custom-call(bf16[2048,768]{1,0:T(8,128)(2,1)} %x_ref.5, s32[2,1,1024]{2,1,0:T(1,128)} %reshape.58.seg_ref, f32[2,768]{1,0:T(2,128)} %gain_ref.7, ...), custom_call_target="tpu_custom_call" | custom-call | tf_op jit(solution)/shard_map/attend/pallas_call | solution.py:157
  268.0 10.2 %mix.1 = (f32[2048,768]{1,0:T(8,128)}, bf16[2048,768]{1,0:T(8,128)(2,1)}) custom-call(bf16[2048,768]{1,0:T(8,128)(2,1)} %x_ref.5, bf16[768,2048]{1,0:T(8,128)(2,1)} %get-tuple-element.36.ot_ref, bf16[768,768]{1,0:T(8,128)(2,1)} %shard_map.204.wo_ref, f32[2,768]{1,0:T(2,128)} %bias_ref.3, f32[2,768]{1,0:T(2,128)} %gain_ref.7, f32[2,768]{1,0:T(2,128)} %shift_ref.3), custom_call_target="tpu_custom_call" | custom-call | tf_op jit(solution)/shard_map/mix/pallas_call | solution.py:275
  278.2 64.4 %mlp.1 = (f32[2048,768]{1,0:T(8,128)}, f32[2048,768]{1,0:T(8,128)}, f32[768,768]{1,0:T(8,128)}, f32[768,768]{1,0:T(8,128)}, f32[1,768]{1,0:T(1,128)}) custom-call(s32[1]{0:T(128)} %bitcast.me_ref, bf16[2048,768]{1,0:T(8,128)(2,1)} %get-tuple-element.38.h2_ref, bf16[2048,768]{1,0:T(8,128)(2,1)} %g_ref.3, f32[4,768,768]{2,1,0:T(8,128)} %get-tuple-element.72.up_ref, ...), custom_call_target="tpu_custom_call" | custom-call | tf_op jit(solution)/shard_map/mlp/pallas_call | solution.py:348
  342.6 16.7 %mix_back.1 = (bf16[2048,768]{1,0:T(8,128)(2,1)}, f32[2048,768]{1,0:T(8,128)}, bf16[768,2048]{1,0:T(8,128)(2,1)}, f32[192,768]{1,0:T(8,128)}, f32[8,768]{1,0:T(8,128)}) custom-call(s32[1]{0:T(128)} %bitcast.me_ref, f32[2048,768]{1,0:T(8,128)} %get-tuple-element.37.mixed_ref, f32[2048,768]{1,0:T(8,128)} %get-tuple-element.39.res_ref, ...), custom_call_target="tpu_custom_call" | custom-call | tf_op jit(solution)/shard_map/mix_back/pallas_call | solution.py:403
  359.3 60.3 %attend_back.1 = (bf16[768,2048]{1,0:T(8,128)(2,1)}, bf16[768,2048]{1,0:T(8,128)(2,1)}, bf16[768,2048]{1,0:T(8,128)(2,1)}) custom-call(s32[1]{0:T(128)S(6)} %mul.7.start_ref, s32[2,1,1024]{2,1,0:T(1,128)} %reshape.58.seg_ref, bf16[768,2048]{1,0:T(8,128)(2,1)} %get-tuple-element.42.qt_ref, bf16[768,2048]{1,0:T(8,128)(2,1)} %get-tuple-element.43.kt_ref, ...), custom_call_target="tpu_custom_call" | custom-call | tf_op jit(solution)/shard_map/attend_back/pallas_call | solution.py:248
  419.5 20.1 %token_back.1 = (f32[2048,768]{1,0:T(8,128)}, f32[3,192,768]{2,1,0:T(8,128)}, f32[8,768]{1,0:T(8,128)}, f32[2,192,128]{2,1,0:T(8,128)}) custom-call(s32[1]{0:T(128)} %bitcast.me_ref, bf16[768,2048]{1,0:T(8,128)(2,1)} %get-tuple-element.47.dq_ref.dqo_ref, bf16[768,2048]{1,0:T(8,128)(2,1)} %get-tuple-element.48.dk_ref.dko_ref, ...), custom_call_target="tpu_custom_call" | custom-call | tf_op jit(solution)/shard_map/token_back/pallas_call | solution.py:454
  439.7 0.0 copy-start.5
  439.7 0.0 copy-start.7
  439.7 0.0 copy-start.3
  439.7 0.0 all-reduce.5.cloned.1.call-update
  439.7 0.8 slice.58
  440.6 0.0 copy-done.5
  440.6 0.0 copy-done.7
  440.6 0.1 copy-done.3
  440.7 0.1 slice_reduce_fusion
  440.8 25.5 %all-reduce.1 = (f32[4,768]{1,0:T(4,128)S(1)}, f32[2,768]{1,0:T(2,128)S(1)}, f32[2,192]{1,0:T(2,128)}, f32[768]{0:T(1024)}) all-reduce(f32[4,768]{1,0:T(4,128)S(1)} %slice.60, f32[2,768]{1,0:T(2,128)S(1)} %slice.58, f32[2,192]{1,0:T(2,128)S(1)} %slice_reduce_fusion, f32[768]{0:T(1024)S(1)} %reduce.3), channel_id=1, replica_groups=mesh['dp'=8,'mp'=4] {'dp'}, use_global_device_ids=true, to_apply=%region_1.2 | all-reduce | flops 5760 | bytes 46080 | tf_op jit(solution)/shard_map/psum | solution.py:522
  466.3 0.6 slice.78
  466.9 0.6 pad_maximum_fusion.2
  467.5 0.6 pad_maximum_fusion.1
  468.1 83.8 %all-reduce.5.cloned.1.call-done = (f32[3,768,192]{1,2,0:T(8,128)}, f32[192,768]{1,0:T(8,128)}, f32[768,768]{1,0:T(8,128)}, f32[768,768]{1,0:T(8,128)}) async-done(((f32[3,768,192]{1,2,0:T(8,128)}, f32[192,768]{1,0:T(8,128)}, f32[768,768]{1,0:T(8,128)}, f32[768,768]{1,0:T(8,128)}), (f32[3,768,192]{1,2,0:T(8,128)}, f32[192,768]{1,0:T(8,128)}, f32[768,768]{1,0:T(8,128)}, ...) | async-done | bytes 7077904 | tf_op jit(solution)/shard_map/psum | solution.py:522
  551.9 2.9 copy.32
  554.8 0.0 copy-done.2
  554.9 0.8 copy.33
  555.7 1.4 copy.34
  557.1 1.4 copy.35
  (14 shorter events, 0.1 us)
Async XLA Ops:
  7.2 176.8 %all-gather.4.cloned.1.call-start = ((), (), s32[]{:S(2)}) async-start(), calls=%async_computation | async-start | bytes 29196288 | tf_op jit(solution)/shard_map/all_gather | solution.py:498
  7.2 2.6 copy-start.6
  7.2 2.7 copy-start.4
  7.3 3.3 copy-start.8
  9.8 542.1 %all-reduce.5.cloned.1.call-start = ((), (), s32[]{:S(2)}) async-start(), calls=%async_computation.1 | async-start | bytes 14155776 | tf_op jit(solution)/shard_map/psum | solution.py:522
  439.7 0.9 copy-start.5
  439.7 0.9 copy-start.7
  439.7 1.0 copy-start.3
  551.9 3.0 copy-start.2
  551.9 3.8 copy-start.1
  554.9 2.2 copy-start
Sparse Core Ops, SparseCore 0:
  11.5 172.4 all-gather.3
  439.9 111.9 all-reduce.4

commit v2 on v1

--- a/solution.py
+++ b/solution.py
@@ -54,20 +54,255 @@
     return jax.ShapeDtypeStruct(shape, dtype)
 
 
-def cast_kernel(in_ref, out_ref):
-    out_ref[...] = in_ref[...].astype(BF)
-
-
-def cast_low(array):
-    rows, width = array.shape
-    block = pl.BlockSpec((256, width), lambda i: (i, 0))
+def flip(index, bit):
+    return index + bit - 2 * bit * lax.rem(lax.div(index, bit), 2)
+
+
+def remote(src, dst, send_sem, recv_sem, **where):
+    return pltpu.make_async_remote_copy(
+        src_ref=src, dst_ref=dst, send_sem=send_sem, recv_sem=recv_sem, device_id=where,
+        device_id_type=pl.DeviceIdType.MESH,
+    )
+
+
+CORE, SIDE, ACROSS, DIAG_A, DIAG_B, CORE_SIDE, CORE_ACROSS, CORE_A, CORE_B = range(9)
+
+
+class Spread:
+    def __init__(self, piece, send_sems, recv_sems, mine=None):
+        self.piece, self.send_sems, self.recv_sems, self.mine = piece, send_sems, recv_sems, mine
+        self.device = lax.axis_index("dp")
+        self.place = lax.rem(self.device, 8)
+
+    def copy(self, chunk, kind, origin, bit, half=None):
+        ref = self.piece(chunk, origin, half)
+        own = self.mine is not None and kind in (CORE, SIDE, ACROSS)
+        return remote(
+            self.mine(chunk) if own else ref, ref, self.send_sems.at[chunk, kind], self.recv_sems.at[chunk, kind], dp=flip(self.device, bit)
+        )
+
+    def origin(self, bits):
+        place = self.place
+        for bit in bits:
+            place = flip(place, bit)
+        return place
+
+    def outgoing(self, chunk, kind):
+        bits, bit, half = {
+            CORE: ((), 1, None),
+            SIDE: ((), 2, None),
+            ACROSS: ((), 4, None),
+            DIAG_A: ((2,), 4, 0),
+            DIAG_B: ((4,), 2, 1),
+            CORE_SIDE: ((2,), 1, None),
+            CORE_ACROSS: ((4,), 1, None),
+            CORE_A: ((2, 4), 1, 0),
+            CORE_B: ((2, 4), 1, 1),
+        }[kind]
+        return self.copy(chunk, kind, self.origin(bits), bit, half)
+
+    def incoming(self, chunk, kind):
+        bits, bit, half = {
+            CORE: ((1,), 1, None),
+            SIDE: ((2,), 2, None),
+            ACROSS: ((4,), 4, None),
+            DIAG_A: ((2, 4), 4, 0),
+            DIAG_B: ((2, 4), 2, 1),
+            CORE_SIDE: ((1, 2), 1, None),
+            CORE_ACROSS: ((1, 4), 1, None),
+            CORE_A: ((1, 2, 4), 1, 0),
+            CORE_B: ((1, 2, 4), 1, 1),
+        }[kind]
+        return self.copy(chunk, kind, self.origin(bits), bit, half)
+
+    def start(self, chunk, *kinds):
+        for kind in kinds:
+            self.outgoing(chunk, kind).start()
+
+    def arrived(self, chunk, *kinds):
+        for kind in kinds:
+            self.incoming(chunk, kind).wait_recv()
+
+    def send(self, chunk):
+        self.start(chunk, SIDE, ACROSS, CORE)
+
+    def forward(self, chunk):
+        self.arrived(chunk, SIDE)
+        self.start(chunk, DIAG_A, CORE_SIDE)
+        self.arrived(chunk, ACROSS)
+        self.start(chunk, DIAG_B, CORE_ACROSS)
+
+    def corner(self, chunk):
+        self.arrived(chunk, DIAG_A)
+        self.start(chunk, CORE_A)
+        self.arrived(chunk, DIAG_B)
+        self.start(chunk, CORE_B)
+
+    def complete(self, chunk):
+        self.arrived(chunk, CORE, CORE_SIDE, CORE_ACROSS, CORE_A, CORE_B)
+
+    def sent(self, chunk):
+        for kind in range(9):
+            self.outgoing(chunk, kind).wait_send()
+
+
+def greet(*peers):
+    barrier = pltpu.get_barrier_semaphore()
+    for peer in peers:
+        pl.semaphore_signal(barrier, inc=1, device_id=peer, device_id_type=pl.DeviceIdType.MESH)
+    pl.semaphore_wait(barrier, len(peers))
+
+
+def foreign_order(me):
+    half = lax.div(me, 2)
+    return flip(me, 1), 2 - half, 3 - 3 * half
+
+
+def gather_kernel(
+    slab_ref, small_ref, w_ref, bias_ref, smalls_ref,
+    land, small_land, z_send, z_recv, own_send, small_send, small_recv, send_sems, recv_sems,
+):
+    parts, rows, width = land.shape
+    own = rows // 3
+    share = rows // 8
+    split = (0, share // 2 + 4, share)
+    me = lax.axis_index("mp")
+    device = lax.axis_index("dp")
+    greet(
+        *[{"mp": lax.rem(me + s, parts)} for s in range(1, parts)],
+        *[{"dp": flip(device, bit)} for bit in (1, 2, 4)],
+    )
+    order = foreign_order(me)
+
+    def rows_of(c, origin, half=None):
+        start, stop = split[c % 2], split[c % 2 + 1]
+        middle = start + (stop - start + 8) // 16 * 8
+        if half is not None:
+            start, stop = (start, middle) if half == 0 else (middle, stop)
+        return pl.ds(pl.multiple_of(origin * share + start, 8), stop - start)
+
+    def piece(c, origin, half):
+        return land.at[order[c // 2], rows_of(c, origin, half), :]
+
+    spread = Spread(piece, send_sems, recv_sems)
+
+    def own_copy(h, up):
+        rows = rows_of(h, spread.place)
+        return remote(
+            slab_ref.at[rows, :], land.at[me, rows, :], own_send.at[h, up], z_recv.at[me * 2 + h], mp=me + 2 * up - 1
+        )
+
+    def on_copy(c, step):
+        ref = piece(c, spread.place, None)
+        chunk = order[c // 2] * 2 + c % 2
+        return remote(ref, ref, z_send.at[chunk], z_recv.at[chunk], mp=me + step)
+
+    for h in range(2):
+        @pl.when(me < parts - 1)
+        def _():
+            own_copy(h, 1).start()
+
+        @pl.when(me > 0)
+        def _():
+            own_copy(h, 0).start()
+
+    def small_copy(s):
+        return remote(
+            small_ref, small_land.at[me], small_send.at[s - 1], small_recv.at[me], mp=lax.rem(me + s, parts)
+        )
+
+    for s in range(1, parts):
+        small_copy(s).start()
+
+    def pass_on(c, act):
+        source = order[c // 2]
+
+        @pl.when((source < me) & (me < parts - 1))
+        def _():
+            act(on_copy(c, 1))
+
+        @pl.when((source > me) & (me > 0))
+        def _():
+            act(on_copy(c, -1))
+
+    def landed(c):
+        on_copy(c, 0).wait_recv()
+        pass_on(c, lambda copy: copy.start())
+        spread.send(c)
+
+    def use(source, ref):
+        for j in range(3):
+            at = pl.multiple_of((j * parts + lax.rem(source - me + parts, parts)) * own, own)
+            w_ref[pl.ds(at, own), :] = ref[j * own : (j + 1) * own, :].astype(BF)
+
+    use(me, slab_ref)
+    small_land[me] = small_ref[...]
+    landed(0)
+    landed(1)
+    last = 5
+    for c in range(last + 1):
+        spread.forward(c)
+        if c + 2 <= last:
+            landed(c + 2)
+        if c > 0:
+            spread.corner(c - 1)
+    spread.corner(last)
+    for s in range(1, parts):
+        other = lax.rem(me + s, parts)
+        remote(small_ref, small_land.at[other], small_send.at[0], small_recv.at[other], mp=me).wait_recv()
+    bias_ref[...] = jnp.zeros_like(bias_ref)
+    for source in range(parts):
+        cols = small_land[source].T
+        place = lax.rem(source - me + parts, parts)
+        for j in range(2):
+            at = pl.multiple_of((2 * j * parts + place) * own, own)
+            bias_ref[pl.ds(at, own), :] = cols[:own, j : j + 1]
+    smalls_ref[...] = small_land[...]
+    for j in range(3):
+        for h in range(2):
+            spread.complete(2 * j + h)
+        use(order[j], land.at[order[j]])
+    for c in range(last + 1):
+        spread.sent(c)
+        pass_on(c, lambda copy: copy.wait_send())
+    for s in range(1, parts):
+        small_copy(s).wait_send()
+    for h in range(2):
+        @pl.when(me < parts - 1)
+        def _():
+            own_copy(h, 1).wait_send()
+
+        @pl.when(me > 0)
+        def _():
+            own_copy(h, 0).wait_send()
+
+
+def gather(slab, small, parts):
+    rows, width = slab.shape
+    dma = pltpu.SemaphoreType.DMA
     return pl.pallas_call(
-        cast_kernel,
-        grid=(rows // 256,),
-        in_specs=[block],
-        out_specs=block,
-        out_shape=shape_of(array.shape, BF),
-    )(array)
+        gather_kernel,
+        in_specs=[WHOLE, WHOLE],
+        out_specs=[WHOLE] * 3,
+        out_shape=[
+            shape_of((rows * parts, width), BF),
+            shape_of((rows * parts, 1), F32),
+            shape_of((parts,) + small.shape, F32),
+        ],
+        scratch_shapes=[
+            pltpu.VMEM((parts, rows, width), F32),
+            pltpu.VMEM((parts,) + small.shape, F32),
+            dma((2 * parts,)),
+            dma((2 * parts,)),
+            dma((2, 2)),
+            dma((parts - 1,)),
+            dma((parts,)),
+            dma((2 * parts, 9)),
+            dma((2 * parts, 9)),
+        ],
+        compiler_params=pltpu.CompilerParams(vmem_limit_bytes=56 * 2**20, collective_id=0, has_side_effects=True),
+        name="gather",
+    )(slab, small)
 
 
 def attend_kernel(
@@ -261,28 +496,6 @@
     )(start, seg, qt, kt, vt, ot, dt, lse)
 
 
-def mix_kernel(x_ref, ot_ref, wo_ref, bias_ref, gain_ref, shift_ref, mixed_ref, h2_ref):
-    mixed = x_ref[...].astype(F32) + dot(ot_ref[...], wo_ref[...], TN) + bias_ref[0:1, :]
-    mixed_ref[...] = mixed
-    normed, _ = standardize(mixed)
-    h2_ref[...] = (normed * gain_ref[1:2, :] + shift_ref[1:2, :]).astype(BF)
-
-
-def mix(x, ot, wo, biases, gains, shifts):
-    tokens, width = x.shape
-    row = pl.BlockSpec((TILE, width), lambda t: (t, 0))
-    col = pl.BlockSpec((width, TILE), lambda t: (0, t))
-    return pl.pallas_call(
-        mix_kernel,
-        grid=(tokens // TILE,),
-        in_specs=[row, col, WHOLE, WHOLE, WHOLE, WHOLE],
-        out_specs=[row, row],
-        out_shape=[shape_of((tokens, width), F32), shape_of((tokens, width), BF)],
-        compiler_params=params(),
-        name="mix",
-    )(x, ot, wo, biases, gains, shifts)
-
-
 GELU_C = 0.7978845608028654
 GELU_A = 0.044715
 
@@ -295,129 +508,211 @@
     return act, slope
 
 
+ONCE = pl.BlockSpec(memory_space=pltpu.VMEM, pipeline_mode=pl.Buffered(1))
+ANY = pl.BlockSpec(memory_space=pl.ANY)
+UNIT = 256
+LONG_TILE = 512
+GAIN_TWO, SHIFT_TWO, BIAS_ONE, BIAS_TWO, UP_BIAS = range(5)
+
+
 def mlp_kernel(
-    me_ref, h2_ref, g_ref, up_ref, down_ref, bias_ref,
-    res_ref, hg_ref, upg_ref, downg_ref, upbg_ref,
-    up_low, down_low,
+    x_ref, ot_ref, mine_ref, wo_ref, g_ref, pieces_ref, up_ref, down_ref, smalls_ref, bias_ref, gain_ref, shift_ref,
+    result_ref, mg_ref, dt_ref, grads_ref,
+    land, wo_low, mixed_ref, h2_ref, res_ref, hg_ref, up_low, down_low, local_sems, send_sems, recv_sems,
 ):
-    j = pl.program_id(0)
-    tokens = h2_ref.shape[0]
-    up_low[...] = up_ref[0].astype(BF)
-    down_low[...] = down_ref[0].astype(BF)
-
-    def tiles(own):
+    step = pl.program_id(0)
+    tokens, width = g_ref.shape
+    parts, own, _ = wo_ref.shape
+    ff = up_ref.shape[1]
+    units = ff // UNIT
+    chunks = units * (parts - 1)
+    share = land.shape[2] // 8
+    strip = UNIT // 8
+    tiles = tokens // TILE
+    first = tiles + 1
+    out_at = 2 * ff
+    sums_at = out_at + own
+    me = lax.axis_index("mp")
+    order = foreign_order(me)
+
+    def source_of(chunk):
+        j = lax.div(chunk, units)
+        return jnp.where(j == 0, order[0], jnp.where(j == 1, order[1], order[2]))
+
+    def piece(chunk, origin, half):
+        rows = pl.ds(pl.multiple_of(origin * share, 8), share)
+        if half is None:
+            return land.at[chunk, :, rows, :]
+        return land.at[chunk, half, rows, :]
+
+    def mine(chunk):
+        return pieces_ref.at[source_of(chunk), lax.rem(chunk, units)]
+
+    spread = Spread(piece, send_sems, recv_sems, mine)
+
+    def keep(chunk):
+        return pltpu.make_async_copy(mine(chunk), piece(chunk, spread.place, None), local_sems.at[chunk])
+
+    def serve(ahead):
+        @pl.when(ahead < chunks)
+        def _():
+            spread.forward(ahead)
+
+        @pl.when(ahead + 2 < chunks)
+        def _():
+            spread.send(ahead + 2)
+
+        @pl.when((ahead > 0) & (ahead - 1 < chunks))
+        def _():
+            spread.corner(ahead - 1)
+
+    def unit(bias, grads_at):
         def tile(i, carry):
-            rows = pl.ds(pl.multiple_of(i * TILE, TILE), TILE)
+            rows = pl.ds(pl.multiple_of(i * LONG_TILE, LONG_TILE), LONG_TILE)
             h2 = h2_ref[rows, :]
             g = g_ref[rows, :]
-            pre = dot(h2, up_low[...], NN) + bias_ref[0]
+            pre = dot(h2, up_low[...], NN) + bias
             act, slope = gelu_both(pre)
             act = act.astype(BF)
             pre_grad = (dot(g, down_low[...], NT) * slope).astype(BF)
-            res = dot(act, down_low[...], NN)
-            hg = dot(pre_grad, up_low[...], NT)
-            if own:
-                res_ref[rows, :] = res
-                hg_ref[rows, :] = hg
-                downg_ref[...] += dot(act, g, TN)
-                upg_ref[...] += dot(h2, pre_grad, TN)
-                upbg_ref[...] += jnp.sum(pre_grad.astype(F32), 0, keepdims=True)
-            else:
-                res_ref[rows, :] += res
-                hg_ref[rows, :] += hg
+            res_ref[rows, :] += dot(act, down_low[...], NN)
+            hg_ref[rows, :] += dot(pre_grad, up_low[...], NT)
+            if grads_at is not None:
+                cols = slice(grads_at, grads_at + UNIT)
+                grads_ref[cols, :] += dot(act, g, TN)
+                grads_ref[ff:out_at, cols] += dot(h2, pre_grad, TN)
+                at = sums_at + UP_BIAS
+                grads_ref[at : at + 1, cols] += jnp.sum(pre_grad.astype(F32), 0, keepdims=True)
             return carry
 
-        lax.fori_loop(0, tokens // TILE, tile, 0)
-
-    @pl.when(j == 0)
+        lax.fori_loop(0, tokens // LONG_TILE, tile, 0)
+
+    @pl.when(step == 0)
     def _():
-        upg_ref[...] = jnp.zeros_like(upg_ref)
-        downg_ref[...] = jnp.zeros_like(downg_ref)
-        upbg_ref[...] = jnp.zeros_like(upbg_ref)
-        tiles(True)
-
-    @pl.when(j > 0)
+        greet(*[{"dp": flip(spread.device, bit)} for bit in (1, 2, 4)])
+        spread.send(0)
+        spread.send(1)
+        for c in range(chunks):
+            keep(c).start()
+        for source in range(parts):
+            at = lax.rem(source - me + parts, parts) * own
+            wo_low[pl.ds(pl.multiple_of(at, own), own), :] = wo_ref[source].astype(BF)
+        grads_ref[...] = jnp.zeros_like(grads_ref)
+
+    @pl.when(step < tiles)
     def _():
-        tiles(False)
-
-
-def mlp(me, h2, g, up, down, bias):
-    tokens, width = h2.shape
-    parts, _, ff = up.shape
-    pick = lambda j, me: (lax.rem(me[0] + j, parts), 0, 0)
+        rows = pl.ds(pl.multiple_of(step * TILE, TILE), TILE)
+        mixed = x_ref[...].astype(F32) + dot(ot_ref[...], wo_low[...], TN) + bias_ref[0:1, :]
+        mixed_ref[rows, :] = mixed
+        res_ref[rows, :] = mixed + bias_ref[1:2, :]
+        hg_ref[rows, :] = jnp.zeros((TILE, width), F32)
+        normed, _ = standardize(mixed)
+        h2_ref[rows, :] = (normed * gain_ref[1:2, :] + shift_ref[1:2, :]).astype(BF)
+
+    @pl.when(step == tiles - 1)
+    def _():
+        serve(0)
+
+    @pl.when(step == tiles)
+    def _():
+        for u in range(units):
+            cols = slice(u * UNIT, (u + 1) * UNIT)
+            up_low[...] = up_ref[:, cols].astype(BF)
+            down_low[...] = down_ref[cols, :].astype(BF)
+            unit(smalls_ref[me, 2:3, cols], u * UNIT)
+            if u < 2:
+                serve(u + 1)
+
+    @pl.when((step >= first) & (step < first + chunks))
+    def _():
+        chunk = step - first
+        keep(chunk).wait()
+        spread.complete(chunk)
+        up_low[...] = land[chunk, 0].astype(BF)
+        for q in range(8):
+            for c in range(width // UNIT):
+                at = q * share + c * strip
+                down_low[q * strip : (q + 1) * strip, c * UNIT : (c + 1) * UNIT] = land[
+                    chunk, 1, at : at + strip, :
+                ].astype(BF)
+        cols = pl.ds(pl.multiple_of(lax.rem(chunk, units) * UNIT, UNIT), UNIT)
+        unit(smalls_ref[source_of(chunk), 2:3, cols], None)
+        serve(chunk + 3)
+
+    @pl.when(step >= first + chunks)
+    def _():
+        rows = pl.ds(pl.multiple_of((step - first - chunks) * TILE, TILE), TILE)
+        g = g_ref[rows, :].astype(F32)
+        result_ref[...] = res_ref[rows, :].astype(BF)
+        normed, inv_std = standardize(mixed_ref[rows, :])
+        hg = hg_ref[rows, :]
+        mg = g + norm_back(hg, normed, inv_std, gain_ref[1:2, :])
+        mg_ref[...] = mg
+        low = mg.astype(BF)
+        dt_ref[...] = dot(wo_low[...], low, NT).astype(BF)
+        grads_ref[out_at:sums_at, :] += dot(mine_ref[...], low, NN)
+        for at, value in ((GAIN_TWO, hg * normed), (SHIFT_TWO, hg), (BIAS_ONE, mg), (BIAS_TWO, g)):
+            grads_ref[sums_at + at : sums_at + at + 1, :] += jnp.sum(value, 0, keepdims=True)
+
+    @pl.when(step == first + chunks + tiles - 1)
+    def _():
+        def done(c, carry):
+            spread.sent(c)
+            return carry
+
+        lax.fori_loop(0, chunks, done, 0)
+
+
+def mlp(x, ot, wo, g, pieces, up, down, smalls, biases, gains, shifts):
+    tokens, width = x.shape
+    parts, own, _ = wo.shape
+    ff = up.shape[1]
+    units = ff // UNIT
+    chunks = units * (parts - 1)
+    tiles = tokens // TILE
+    steps = 2 * tiles + 1 + chunks
+    rows = 2 * ff + own
+    rows += -rows % 128 + (128 if rows % 128 > 120 or rows % 128 == 0 else 0)
+    early = lambda s: jnp.minimum(s, tiles - 1)
+    late = lambda s: jnp.maximum(s - (steps - tiles), 0)
+    dma = pltpu.SemaphoreType.DMA
     return pl.pallas_call(
         mlp_kernel,
-        grid_spec=pltpu.PrefetchScalarGridSpec(
-            num_scalar_prefetch=1,
-            grid=(parts,),
-            in_specs=[
-                WHOLE,
-                WHOLE,
-                pl.BlockSpec((1, width, ff), pick),
-                pl.BlockSpec((1, ff, width), pick),
-                pl.BlockSpec((1, 1, ff), pick),
-            ],
-            out_specs=[WHOLE] * 5,
-            scratch_shapes=[pltpu.VMEM((width, ff), BF), pltpu.VMEM((ff, width), BF)],
-        ),
-        out_shape=[
-            shape_of((tokens, width), F32),
-            shape_of((tokens, width), F32),
-            shape_of((width, ff), F32),
-            shape_of((ff, width), F32),
-            shape_of((1, ff), F32),
+        grid=(steps,),
+        in_specs=[
+            pl.BlockSpec((TILE, width), lambda s: (early(s), 0)),
+            pl.BlockSpec((width, TILE), lambda s: (0, early(s))),
+            pl.BlockSpec((own, TILE), lambda s: (0, late(s))),
+            ONCE, ONCE, ANY, ONCE, ONCE, ONCE, ONCE, ONCE, ONCE,
         ],
-        compiler_params=params(),
-        name="mlp",
-    )(me, h2, g, up, down, bias)
-
-
-def mix_back_kernel(
-    me_ref, mixed_ref, res_ref, hg_ref, g_ref, ot_ref, wo_ref, bias_ref, gain_ref,
-    result_ref, mg_ref, dt_ref, owg_ref, sums_ref,
-):
-    @pl.when(pl.program_id(0) == 0)
-    def _():
-        owg_ref[...] = jnp.zeros_like(owg_ref)
-        sums_ref[...] = jnp.zeros_like(sums_ref)
-
-    mixed = mixed_ref[...]
-    g = g_ref[...].astype(F32)
-    result_ref[...] = (mixed + res_ref[...] + bias_ref[1:2, :]).astype(BF)
-    normed, inv_std = standardize(mixed)
-    hg = hg_ref[...]
-    mg = g + norm_back(hg, normed, inv_std, gain_ref[1:2, :])
-    mg_ref[...] = mg
-    low = mg.astype(BF)
-    dt_ref[...] = dot(wo_ref[...], low, NT).astype(BF)
-    owg_ref[...] += dot(ot_ref[...], low, NN)
-    sums_ref[0:1, :] += jnp.sum(hg * normed, 0, keepdims=True)
-    sums_ref[1:2, :] += jnp.sum(hg, 0, keepdims=True)
-    sums_ref[2:3, :] += jnp.sum(mg, 0, keepdims=True)
-    sums_ref[3:4, :] += jnp.sum(g, 0, keepdims=True)
-
-
-def mix_back(me, mixed, res, hg, g, ot, wo, biases, gains, own):
-    tokens, width = mixed.shape
-    row = pl.BlockSpec((TILE, width), lambda t, me: (t, 0))
-    return pl.pallas_call(
-        mix_back_kernel,
-        grid_spec=pltpu.PrefetchScalarGridSpec(
-            num_scalar_prefetch=1,
-            grid=(tokens // TILE,),
-            in_specs=[row, row, row, row, pl.BlockSpec((own, TILE), lambda t, me: (me[0], t)), WHOLE, WHOLE, WHOLE],
-            out_specs=[row, row, pl.BlockSpec((width, TILE), lambda t, me: (0, t)), WHOLE, WHOLE],
-        ),
+        out_specs=[
+            pl.BlockSpec((TILE, width), lambda s: (late(s), 0)),
+            pl.BlockSpec((TILE, width), lambda s: (late(s), 0)),
+            pl.BlockSpec((width, TILE), lambda s: (0, late(s))),
+            ONCE,
+        ],
         out_shape=[
             shape_of((tokens, width), BF),
             shape_of((tokens, width), F32),
             shape_of((width, tokens), BF),
-            shape_of((own, width), F32),
-            shape_of((8, width), F32),
+            shape_of((rows, width), F32),
         ],
-        compiler_params=params(),
-        name="mix_back",
-    )(me, mixed, res, hg, g, ot, wo, biases, gains)
+        scratch_shapes=[
+            pltpu.VMEM((chunks, 2, width, UNIT), F32),
+            pltpu.VMEM((parts * own, width), BF),
+            pltpu.VMEM((tokens, width), F32),
+            pltpu.VMEM((tokens, width), BF),
+            pltpu.VMEM((tokens, width), F32),
+            pltpu.VMEM((tokens, width), F32),
+            pltpu.VMEM((width, UNIT), BF),
+            pltpu.VMEM((UNIT, width), BF),
+            dma((chunks,)),
+            dma((chunks, 9)),
+            dma((chunks, 9)),
+        ],
+        compiler_params=pltpu.CompilerParams(vmem_limit_bytes=63 * 2**20, collective_id=1, has_side_effects=True),
+        name="mlp",
+    )(x, ot, ot, wo, g, pieces, up, down, smalls, biases, gains, shifts)
 
 
 def token_kernel(
@@ -450,7 +745,7 @@
     tokens, width = x.shape
     row = pl.BlockSpec((TILE, width), lambda t, me: (t, 0))
     col = pl.BlockSpec((width, TILE), lambda t, me: (0, t))
-    mine = pl.BlockSpec((own, TILE), lambda t, me: (me[0], t))
+    mine = pl.BlockSpec((own, TILE), lambda t, me: (0, t))
     return pl.pallas_call(
         token_kernel,
         grid_spec=pltpu.PrefetchScalarGridSpec(
@@ -488,40 +783,40 @@
     width = tokens.shape[1]
     own = qkv_weight.shape[2]
     ff = up_weight.shape[1]
+    parts = width // own
     me = lax.axis_index("mp").astype(jnp.int32).reshape(1)
+    place = lax.rem(lax.axis_index("dp"), 8)
     seg = segments.reshape(segments.shape[0], 1, segments.shape[1])
-    slab = jnp.concatenate(
-        [qkv_weight.transpose(0, 2, 1).reshape(3 * own, width), out_weight, up_weight, down_weight], 0
-    )
-    share = slab.shape[0] // dp_size
-    piece = lax.dynamic_slice_in_dim(slab, lax.axis_index("dp") * share, share, 0)
-    gathered = lax.all_gather(piece, ("mp", "dp"), tiled=True).reshape(-1, slab.shape[0], width)
-    small = jnp.concatenate([jnp.pad(qv_bias, ((0, 0), (0, width - own))), up_bias.reshape(1, ff)], 0)
-    smalls = lax.all_gather(small, "mp")
-    parts = gathered.shape[0]
-    qkv_t = gathered[:, : 3 * own].reshape(parts, 3, own, width).transpose(1, 0, 2, 3).reshape(3 * parts * own, width)
-    weights = cast_low(qkv_t)
-    wo = cast_low(gathered[:, 3 * own : 4 * own].reshape(parts * own, width))
-    up = gathered[:, 4 * own : 4 * own + width]
-    down = gathered[:, 4 * own + width :]
-    full_bias = smalls[:, :2, :own].transpose(1, 0, 2).reshape(2, parts * own)
-    bias = jnp.concatenate([full_bias[0], jnp.zeros_like(full_bias[0]), full_bias[1]]).reshape(-1, 1)
+    out_piece = lax.dynamic_slice_in_dim(out_weight, place * (own // 8), own // 8, 0)
+    wo = lax.all_gather(out_piece, ("mp", "dp"), tiled=True) if dp_size == 8 else lax.all_gather(
+        out_weight, "mp", tiled=True
+    )
+    share, units, strip = width // 8, ff // UNIT, UNIT // 8
+    up_piece = lax.dynamic_slice_in_dim(up_weight, place * share, share, 0).reshape(share, units, UNIT)
+    down_piece = lax.dynamic_slice_in_dim(down_weight.reshape(units, 8, strip, -1, UNIT), place, 1, 1)
+    down_piece = down_piece.reshape(units, strip, -1, UNIT).transpose(0, 2, 1, 3).reshape(units, share, UNIT)
+    pieces = lax.all_gather(jnp.stack([up_piece.transpose(1, 0, 2), down_piece], 1), "mp")
+    slab = qkv_weight.transpose(0, 2, 1).reshape(3 * own, width)
+    small = jnp.concatenate(
+        [jnp.pad(qv_bias, ((0, 0), (0, width - own))), up_bias.reshape(1, ff), jnp.zeros((5, width), F32)], 0
+    )
+    weights, bias, smalls = gather(slab, small, parts)
     h1, qt, kt, vt, ot, lse = attend(tokens, seg, norm_gains, norm_shifts, weights, bias)
-    mixed, h2 = mix(tokens, ot, wo, out_biases, norm_gains, norm_shifts)
-    res, hg, up_grad, down_grad, up_bias_grad = mlp(me, h2, cotangent, up, down, smalls[:, 2:3, :])
-    result, mg, dt, out_weight_grad, sums_two = mix_back(
-        me, mixed, res, hg, cotangent, ot, wo, out_biases, norm_gains, own
-    )
-    up_grad, down_grad, out_weight_grad, up_bias_grad = lax.psum(
-        (up_grad, down_grad, out_weight_grad, up_bias_grad), "dp"
-    )
-    dq, dk, dv = attend_back(me * (own // HEAD_DIM), seg, qt, kt, vt, ot, dt, lse)
+    result, mg, dt, grads = mlp(
+        tokens, ot, wo.reshape(parts, own, width), cotangent, pieces, up_weight, down_weight, smalls, out_biases,
+        norm_gains, norm_shifts,
+    )
+    grads = lax.psum(grads, "dp")
+    out_at = 2 * ff
+    sums_at = out_at + own
+    sums_two = grads[sums_at : sums_at + 4]
+    down_grad, up_grad, out_weight_grad = grads[:ff], grads[ff:out_at], grads[out_at:sums_at]
+    up_bias_grad = grads[sums_at + UP_BIAS]
+    dq, dk, dv = attend_back(me * 0, seg, qt, kt, vt, ot, dt, lse)
     token_grad, qkv_grad, sums_one, row_sums = token_back(
         me, dq, dk, dv, weights, tokens, h1, mg, norm_gains, own
     )
-    qkv_grad, sums_one, sums_two, row_sums = lax.psum(
-        (qkv_grad, sums_one[:2], sums_two[:4], row_sums[:, :, 0]), "dp"
-    )
+    qkv_grad, sums_one, row_sums = lax.psum((qkv_grad, sums_one[:2], row_sums[:, :, 0]), "dp")
     return (
         result,
         token_grad,

time: 566 us -> 455 us (0.80)
  waiting for transfers between devices: 240 us -> 115 us
  Pallas kernels: 227 us -> 286 us
  blocking collectives: 40.3 us -> 13.6 us
  local copies, waits for them, and re-layouts: 40.2 us -> 24 us
    all_gather x1 -> x2, waiting for transfers between devices: 157 us -> 13.9 us  [the longest x1 13.9 us: body(): lax.all_gather(out_piece, ('mp', 'dp'), tiled=True)]
    pallas_call x5 -> x2, Pallas kernels: 102 us -> 162 us  [the longest x1 98.3 us: mlp(): pl.pallas_call(mlp_kernel, grid=(steps,), in_specs=[pl.BlockSpec((TILE, w...]
    psum x1, waiting for transfers between devices: 83.8 us -> 101 us  [body(): grads = lax.psum(grads, 'dp')]
    slice x7 -> x4, local copies, waits for them, and re-layouts: 23.4 us -> 8.39 us  [the longest x1 5.02 us: body(): grads[:ff]]
    all_gather x1 -> x0, blocking collectives: 14.7 us -> none  [body(): smalls = lax.all_gather(small, 'mp')]
    psum x1, blocking collectives: 25.5 us -> 13.6 us  [body(): lax.psum((qkv_grad, sums_one[:2], row_sums[:, :, 0]), 'dp')]
    transpose x2 -> x1, local copies, waits for them, and re-layouts: 6.39 us -> 0.21 us  [body(): down_piece.reshape(units, strip, -1, UNIT).transpose(0, 2, 1, 3)]
  transfers between devices with their start and end apart: 2 -> 3, of which waited for: 2 -> 2; matrix products, arithmetic and copies ran while one was open for 1% -> 1% of each run, Pallas kernels for 0% -> 24%
where the time goes in v2:
time: 455 us; the launch traced here: 454 us
  Pallas kernels  286 us (63%)
  waiting for transfers between devices  115 us (25%)
  local copies, waits for them, and re-layouts  24 us (5%)
  between operations  13.9 us (3%)
  blocking collectives  13.6 us (3%)
    psum x1, waiting for transfers between devices, body(): grads = lax.psum(grads, 'dp')  101 us
    pallas_call x1, Pallas kernels, mlp(): pl.pallas_call(mlp_kernel, grid=(steps,), in_specs=[pl.BlockSpec((TILE, w...  98.3 us
    pallas_call x1, Pallas kernels, gather(): pl.pallas_call(gather_kernel, in_specs=[WHOLE, WHOLE], out_specs=[WHOLE]...  63.7 us
    pallas_call x1, Pallas kernels, attend_back(): pl.pallas_call(attend_back_kernel, grid=(rows,), in_specs=[SCALARS, pl.Bl...  60.7 us
    pallas_call x1, Pallas kernels, attend(): pl.pallas_call(attend_kernel, grid=(rows,), in_specs=[row, pl.BlockSpec((...  43.8 us
    pallas_call x1, Pallas kernels, token_back(): pl.pallas_call(token_kernel, grid_spec=pltpu.PrefetchScalarGridSpec(num_s...  19.9 us
    all_gather x1, waiting for transfers between devices, body(): lax.all_gather(out_piece, ('mp', 'dp'), tiled=True)  13.9 us
    psum x1, blocking collectives, body(): lax.psum((qkv_grad, sums_one[:2], row_sums[:, :, 0]), 'dp')  13.6 us
  transfers between devices with their start and end apart: 3, of which 2 were waited for; matrix products, arithmetic and copies ran while one was open for 1% of the time, Pallas kernels for 24%

profile of v2, /device:TPU:0, one launch (start us, length us, event | category | flops | bytes accessed | tf_op | source)
XLA Modules:
  0.0 453.9 jit_solution(9300659912101806074)
XLA Ops:
  7.2 0.0 copy-start
  7.2 0.0 all-gather.6.cloned.1.call-start
  7.3 1.0 constant_dynamic-slice_fusion.1
  8.3 0.2 reshape.50
  8.5 4.5 reshape.51
  13.0 0.0 copy-start.6
  13.0 0.0 copy-start.5
  13.0 1.1 constant_dynamic-slice_fusion
  14.1 0.1 copy.30
  14.2 0.2 copy.27
  14.4 0.2 pad_maximum_fusion
  14.6 0.9 copy.28
  15.5 0.0 all-gather.6.cloned.1.call-update
  15.5 0.0 all-gather.4.cloned.1.call-start
  15.6 0.0 copy-done
  15.6 0.6 constant_dynamic-slice_fusion.2
  16.2 0.0 all-gather.4.cloned.1.call-update
  16.3 0.0 all-reduce.5.cloned.1.call-start
  16.3 0.0 copy-done.6
  16.3 0.0 copy-done.5
  16.3 0.6 reshape.46.seg_ref
  16.9 0.1 pad.13.clone
  17.0 0.0 copy-done.7
  17.0 0.7 fusion.small_ref
  17.7 63.7 %gather.1 = (bf16[2304,768]{1,0:T(8,128)(2,1)}, f32[2304,1]{1,0:T(8,128)}, f32[4,8,768]{2,1,0:T(8,128)}) custom-call(f32[576,768]{1,0:T(8,128)} %bitcast.19, f32[8,768]{1,0:T(8,128)} %fusion.small_ref), custom_call_target="tpu_custom_call" | custom-call | tf_op jit(solution)/shard_map/gather/pallas_call | solution.py:283
  81.4 43.8 %attend.1 = (bf16[2048,768]{1,0:T(8,128)(2,1)}, bf16[768,2048]{1,0:T(8,128)(2,1)}, bf16[768,2048]{1,0:T(8,128)(2,1)}, bf16[768,2048]{1,0:T(8,128)(2,1)}, bf16[768,2048]{1,0:T(8,128)(2,1)}, /*index=5*/f32[16,2048]{1,0:T(8,128)}) custom-call(bf16[2048,768]{1,0:T(8,128)(2,1)} %x_ref.5, s32[2,1,1024]{2,1,0:T(1,128)} %reshape.46.seg_ref, f32[2,768]{1,0:T(2,128)} %gain_ref.5, ...), custom_call_target="tpu_custom_call" | custom-call | tf_op jit(solution)/shard_map/attend/pallas_call | solution.py:392
  125.2 0.0 all-gather.6.cloned.1.call-done
  125.3 13.9 %all-gather.4.cloned.1.call-done = f32[768,768]{1,0:T(8,128)} async-done(((f32[24,768]{1,0:T(8,128)}), f32[768,768]{1,0:T(8,128)}) %all-gather.4.cloned.1.call-update) | async-done | bytes 2359312 | tf_op jit(solution)/shard_map/all_gather | solution.py:791
  139.2 98.3 %mlp.1 = (bf16[2048,768]{1,0:T(8,128)(2,1)}, f32[2048,768]{1,0:T(8,128)}, bf16[768,2048]{1,0:T(8,128)(2,1)}, f32[1792,768]{1,0:T(8,128)}) custom-call(bf16[2048,768]{1,0:T(8,128)(2,1)} %x_ref.5, bf16[768,2048]{1,0:T(8,128)(2,1)} %get-tuple-element.33.ot_ref.mine_ref, bf16[768,2048]{1,0:T(8,128)(2,1)} %get-tuple-element.33.ot_ref.mine_ref, ...), custom_call_target="tpu_custom_call" | custom-call | tf_op jit(solution)/shard_map/mlp/pallas_call | solution.py:679
  237.5 60.7 %attend_back.1 = (bf16[768,2048]{1,0:T(8,128)(2,1)}, bf16[768,2048]{1,0:T(8,128)(2,1)}, bf16[768,2048]{1,0:T(8,128)(2,1)}) custom-call(s32[1]{0:T(128)} %constant.28.clone.1.start_ref, s32[2,1,1024]{2,1,0:T(1,128)} %reshape.46.seg_ref, bf16[768,2048]{1,0:T(8,128)(2,1)} %get-tuple-element.36.qt_ref, bf16[768,2048]{1,0:T(8,128)(2,1)} %get-tuple-element.37.kt_ref, ...), custom_call_target="tpu_custom_call" | custom-call | tf_op jit(solution)/shard_map/attend_back/pallas_call | solution.py:483
  298.1 19.9 %token_back.1 = (f32[2048,768]{1,0:T(8,128)}, f32[3,192,768]{2,1,0:T(8,128)}, f32[8,768]{1,0:T(8,128)}, f32[2,192,128]{2,1,0:T(8,128)}) custom-call(s32[1]{0:T(128)} %bitcast.9.me_ref, bf16[768,2048]{1,0:T(8,128)(2,1)} %get-tuple-element.41.dq_ref.dqo_ref, bf16[768,2048]{1,0:T(8,128)(2,1)} %get-tuple-element.42.dk_ref.dko_ref, ...), custom_call_target="tpu_custom_call" | custom-call | tf_op jit(solution)/shard_map/token_back/pallas_call | solution.py:749
  318.1 0.0 copy-start.4
  318.1 0.0 all-reduce.5.cloned.1.call-update
  318.1 0.8 slice.37
  318.9 0.1 copy-done.4
  319.0 0.1 slice_reduce_fusion
  319.1 13.6 %all-reduce.1 = (f32[2,768]{1,0:T(2,128)S(1)}, f32[2,192]{1,0:T(2,128)}) all-reduce(f32[2,768]{1,0:T(2,128)S(1)} %slice.37, f32[2,192]{1,0:T(2,128)S(1)} %slice_reduce_fusion), channel_id=1, replica_groups=mesh['dp'=8,'mp'=4] {'dp'}, use_global_device_ids=true, to_apply=%region_0.1 | all-reduce | flops 1920 | bytes 15360 | tf_op jit(solution)/shard_map/psum | solution.py:819
  332.7 100.5 %all-reduce.5.cloned.1.call-done = (f32[1792,768]{1,0:T(8,128)}, f32[3,768,192]{1,2,0:T(8,128)}) async-done(((f32[1792,768]{1,0:T(8,128)}, f32[3,768,192]{1,2,0:T(8,128)}), (f32[1792,768]{1,0:T(8,128)}, f32[3,768,192]{1,2,0:T(8,128)})) %all-reduce.5.cloned.1.call-update) | async-done | bytes 7274512 | tf_op jit(solution)/shard_map/psum | solution.py:809
  433.2 1.3 slice.53
  434.6 1.5 slice_reduce_fusion.1
  436.0 1.9 slice.52
  437.9 5.0 %fusion.1 = (f32[768,768]{1,0:T(8,128)}, f32[768,768]{1,0:T(8,128)}) fusion(f32[1792,768]{1,0:T(8,128)} %get-tuple-element.53), kind=kLoop, calls=%fused_computation.12 | loop fusion | bytes 9437184 | tf_op jit(solution)/shard_map/slice | solution.py:813
  442.9 0.6 pad_maximum_fusion.1
  443.5 0.0 copy-done.2
  443.6 1.7 copy.34
  445.2 0.9 copy-done.3
  446.2 1.2 copy.35
  447.4 0.0 copy-done.1
  (7 shorter events, 0.0 us)
Async XLA Ops:
  7.2 8.4 %copy-start = (f32[192,768]{1,0:T(8,128)S(1)}, f32[192,768]{1,0:T(8,128)}, u32[]{:S(2)}) copy-start(f32[192,768]{1,0:T(8,128)} %param.18) | copy-start | bytes 1769476
  7.2 118.1 %all-gather.6.cloned.1.call-start = ((), (), s32[]{:S(2)}) async-start(), calls=%async_computation.1 | async-start | bytes 2949120 | tf_op jit(solution)/shard_map/all_gather | solution.py:798
  13.0 3.3 copy-start.6
  13.0 3.3 copy-start.5
  13.0 4.0 copy-start.7
  15.5 123.7 %all-gather.4.cloned.1.call-start = ((), (), s32[]{:S(2)}) async-start(), calls=%async_computation | async-start | bytes 2433024 | tf_op jit(solution)/shard_map/all_gather | solution.py:791
  16.3 417.0 %all-reduce.5.cloned.1.call-start = ((), (), s32[]{:S(2)}) async-start(), calls=%async_computation.2 | async-start | bytes 14548992 | tf_op jit(solution)/shard_map/psum | solution.py:809
  318.1 0.9 copy-start.4
  437.9 5.6 %copy-start.2 = (bf16[2048,768]{1,0:T(8,128)(2,1)S(1)}, bf16[2048,768]{1,0:T(8,128)(2,1)}, u32[]{:S(2)}) copy-start(bf16[2048,768]{1,0:T(8,128)(2,1)} %get-tuple-element.75) | copy-start | bytes 9437188
  443.6 2.6 copy-start.3
  443.6 3.8 copy-start.1
Sparse Core Ops, SparseCore 0:
  15.6 63.6 all-gather.5
  82.8 56.3 all-gather.3
  318.2 114.9 all-reduce.4
